TPU v7x, 32 devices: a whole 2x2x4 slice. The times are simulated.
32 devices in a mesh: grp: 16 (over z, x, core), span: 2 (over y).
Axes of the slice: x: 2, y: 2, z: 4, core: 2. Of those that a mesh axis runs over, the one named last changes fastest.
Arguments:
- queries: bfloat16 [4096, 2240], P(('grp', 'span')), may hold values from -6 to 6
- key_rows: bfloat16 [4096, 2240], P(('grp', 'span')), may hold values from -6 to 6
- value_rows: bfloat16 [4096, 2240], P(('grp', 'span')), may hold values from -6 to 6
- retention: float32 [32, 20], P(('grp', 'span')), may hold values from 0.2 to 1, as said below
- up_weight: bfloat16 [2240, 2, 3072], P('grp', None, 'span'), may hold values from -0.125 to 0.125
- conv_weight: bfloat16 [3, 3, 3, 2, 3072], P(None, None, None, None, 'span'), may hold values from -1.25 to 1.25
- conv_bias: float32 [2, 3072], P(None, 'span'), may hold values from -3 to 3
Outputs:
- hidden: bfloat16 [4096, 3072], P('grp', 'span')
Inputs may be any that keep to these rules, and one draw needn't show every extreme that they name: `retention`: retention factors of a head's carried state, one per time span.
All inputs are finite; a program needn't handle non-finite values.
Results may differ from a plain program's by a relative error of at most 0.015.
Values may be sent and summed in bfloat16 or wider, within the bound.
A program may use at most 128 MiB of HBM per device.

v0:
```python
import jax
import jax.numpy as jnp
from jax import lax
from jax.sharding import PartitionSpec as P

FH = 8
FW = 16


def prefix_2(x, axis, join, neutral):
    place = lax.axis_index(axis)
    gathered = jax.tree.map(
        lambda a, kind: lax.all_gather(a.astype(kind), axis),
        x,
        jax.tree.map(lambda a: jnp.bfloat16 if a.dtype == jnp.float32 else a.dtype, x),
    )
    state = jax.tree.map(lambda a, e: jnp.zeros_like(a) + jnp.asarray(e, a.dtype), x, neutral)

    def one(hop, state):
        return join(
            state,
            jax.tree.map(
                lambda a, own: lax.dynamic_index_in_dim(a, hop, 0, False).astype(own.dtype),
                gathered,
                x,
            ),
        )

    return lax.fori_loop(0, place, one, state)


def as_sent(x):

    def short(part):
        return part.astype(jnp.bfloat16) if part.dtype == jnp.float32 else part

    return jax.tree.map(short, x)


def extended_2(x, sides, width):
    for axis, dim in sides:
        peers, length = (lax.axis_size(axis), x.shape[dim])
        up = [(i, (i + 1) % peers) for i in range(peers - 1)]
        down = [(j, i) for i, j in up]
        last = lax.slice_in_dim(x, length - width, length, axis=dim)
        initial = lax.slice_in_dim(x, 0, width, axis=dim)
        before = lax.ppermute(last, axis, up)
        after = lax.ppermute(initial, axis, down)
        x = jnp.concatenate([before, x, after], axis=dim)
    return x


def combine(earlier, later):
    factor_e, state_e, sum_e = earlier
    factor_l, state_l, sum_l = later
    return (
        factor_e * factor_l,
        factor_l[:, None, None] * state_e + state_l,
        factor_l[:, None] * sum_e + sum_l,
    )


def shards(queries, key_rows, value_rows, retention, up_weight, conv_weight, conv_bias):
    tokens = queries.shape[0]
    heads = retention.shape[1]
    head_dim = queries.shape[1] // heads
    q_heads = jnp.maximum(queries, 0).reshape(tokens, heads, head_dim)
    k_heads = jnp.maximum(key_rows, 0).reshape(tokens, heads, head_dim)
    v_heads = value_rows.reshape(tokens, heads, head_dim)
    local_state = jnp.einsum("thd,the->hde", k_heads, v_heads, preferred_element_type=jnp.float32)
    local_sum = jnp.sum(k_heads.astype(jnp.float32), axis=0)
    factor = retention[0]
    members = lax.axis_size("span")
    share = head_dim // members
    slice_identity = (
        jnp.ones((heads,), jnp.float32),
        jnp.zeros((heads, share, head_dim), jnp.float32),
        jnp.zeros((heads, share), jnp.float32),
    )
    outgoing_memory = local_state.reshape(heads, members, share, head_dim).transpose(1, 0, 2, 3)
    send_sum = local_sum.reshape(heads, members, share).transpose(1, 0, 2)
    send_factor = jnp.broadcast_to(factor, (members, heads))
    got_factor, got_state, got_sum = (
        lax.all_to_all(send_factor, "span", split_axis=0, concat_axis=0, tiled=True),
        lax.all_to_all(outgoing_memory, "span", split_axis=0, concat_axis=0, tiled=True),
        lax.all_to_all(send_sum, "span", split_axis=0, concat_axis=0, tiled=True),
    )
    running = slice_identity
    prefixes = []
    for member in range(members):
        prefixes.append(running)
        running = combine(running, (got_factor[member], got_state[member], got_sum[member]))
    earlier = prefix_2(running, "grp", combine, slice_identity)
    joined_prefix = [combine(earlier, prefix) for prefix in prefixes]
    stack_state = jnp.stack([item[1] for item in joined_prefix], axis=0)
    stack_sum = jnp.stack([item[2] for item in joined_prefix], axis=0)
    back_state, back_sum = (
        lax.all_to_all(
            as_sent(stack_state), "span", split_axis=0, concat_axis=0, tiled=True
        ).astype(stack_state.dtype),
        lax.all_to_all(as_sent(stack_sum), "span", split_axis=0, concat_axis=0, tiled=True).astype(
            stack_sum.dtype
        ),
    )
    before_state = back_state.transpose(1, 0, 2, 3).reshape(heads, head_dim, head_dim)
    before_sum = back_sum.transpose(1, 0, 2).reshape(heads, head_dim)
    state = factor[:, None, None] * before_state + local_state
    key_sum = factor[:, None] * before_sum + local_sum
    q_float = q_heads.astype(jnp.float32)
    numer = jnp.einsum("thd,hde->the", q_float, state, precision=lax.Precision.HIGHEST)
    denom = jnp.einsum("thd,hd->th", q_float, key_sum, precision=lax.Precision.HIGHEST) + 0.0001
    attended = (numer / denom[:, :, None]).reshape(tokens, heads * head_dim)
    scale = lax.rsqrt(jnp.mean(attended * attended, axis=-1, keepdims=True) + 1e-06)
    normed = (attended * scale).astype(jnp.bfloat16)
    width = up_weight.shape[2]
    full_weight = lax.all_gather(up_weight, "grp", axis=0, tiled=True)
    flat_weight = full_weight.reshape(full_weight.shape[0], 2 * width)
    up_vals = jnp.dot(
        lax.all_gather(normed, "span", axis=0, tiled=True),
        flat_weight,
        preferred_element_type=jnp.float32,
    ).astype(jnp.bfloat16)
    frames = up_vals.shape[0] // (FH * FW)
    grid = up_vals.reshape(frames, FH, FW, 2 * width)
    extended = extended_2(grid, (("grp", 0),), 1)
    padded = jnp.pad(extended, ((0, 0), (1, 1), (1, 1), (0, 0)))
    convolution_kernel = conv_weight.reshape(3, 3, 3, 2 * width).astype(jnp.float32)
    mixed = jnp.zeros((frames, FH, FW, 2 * width), jnp.float32) + conv_bias.reshape(2 * width)
    for tap_t in range(3):
        for tap_y in range(3):
            for tap_x in range(3):
                visible_extent = padded[
                    tap_t : tap_t + frames, tap_y : tap_y + FH, tap_x : tap_x + FW
                ]
                mixed = (
                    mixed
                    + visible_extent.astype(jnp.float32) * convolution_kernel[tap_t, tap_y, tap_x]
                )
    mixed = mixed.reshape(frames * FH * FW, 2, width)
    return (mixed[:, 0] * jax.nn.silu(mixed[:, 1])).astype(jnp.bfloat16)


def solution(mesh):
    in_specs = (
        P(("grp", "span"), None),
        P(("grp", "span"), None),
        P(("grp", "span"), None),
        P(("grp", "span"), None),
        P("grp", None, "span"),
        P(None, None, None, None, "span"),
        P(None, "span"),
    )
    out_specs = P("grp", "span")
    return jax.shard_map(shards, mesh=mesh, in_specs=in_specs, out_specs=out_specs, check_vma=False)
```

profile of v0, /device:TPU:1, one launch (start us, length us, event | category | flops | bytes accessed | tf_op | source)
XLA Modules:
  0.0 288.1 jit_solution(4446213974563162959)
XLA Ops:
  6.5 1.3 broadcast_in_dim.19
  7.8 3.3 %all-to-all-start = ((f32[2,1,20]{2,1,0:T(1,128)}), f32[2,1,20]{2,1,0:T(1,128)S(1)}, u32[]{:S(2)}, u32[]{:S(2)}) async-start(f32[2,1,20]{2,1,0:T(1,128)} %broadcast_in_dim.19), calls=%async_computation | async-start | bytes 2048 | tf_op jit(solution)/shard_map/all_to_all | solution.py:84
  11.2 1.1 broadcast_maximum_fusion.1
  12.3 0.5 fusion.31
  12.7 1.1 copy.47
  13.8 0.3 all-to-all-done
  14.1 3.6 %all-to-all-start.1 = ((f32[2,20,56,112]{3,2,1,0:T(8,128)}), f32[2,20,56,112]{3,2,1,0:T(8,128)S(1)}, u32[]{:S(2)}, u32[]{:S(2)}) async-start(f32[2,20,56,112]{3,2,1,0:T(8,128)} %bitcast.149), calls=%async_computation.1 | async-start | bytes 2293760 | tf_op jit(solution)/shard_map/all_to_all | solution.py:85
  17.8 0.5 slice_bitcast_fusion.1
  18.3 12.8 %all-to-all-done.1 = f32[2,20,56,112]{3,2,1,0:T(8,128)S(1)} async-done(((f32[2,20,56,112]{3,2,1,0:T(8,128)}), f32[2,20,56,112]{3,2,1,0:T(8,128)S(1)}, u32[]{:S(2)}, u32[]{:S(2)}) %all-to-all-start.1) | async-done | bytes 1003552 | tf_op jit(solution)/shard_map/all_to_all | solution.py:85
  31.1 0.9 fusion.16
  32.1 0.7 all-gather.9.cloned.1.call-update
  32.8 0.3 convert_reduce_fusion
  33.0 0.1 reshape.124
  33.1 0.7 reshape.149
  33.8 3.2 %all-to-all-start.2 = ((f32[2,1,1120]{2,1,0:T(1,128)}), f32[2,1,1120]{2,1,0:T(1,128)S(1)}, u32[]{:S(2)}, u32[]{:S(2)}) async-start(f32[2,1,1120]{2,1,0:T(1,128)} %reshape.149), calls=%async_computation.2 | async-start | bytes 18432 | tf_op jit(solution)/shard_map/all_to_all | solution.py:86
  37.1 1.1 broadcast_maximum_fusion
  38.2 0.7 reduce_sum.21
  38.8 23.9 %all-gather = bf16[16,1,20]{2,1,0:T(2,128)(2,1)S(1)} all-gather(bf16[1,1,20]{2,1,0:T(2,128)(2,1)S(1)} %get-tuple-element.124), channel_id=2, replica_groups=mesh['grp'=16,'span'=2] {'grp'}, dimensions={0}, use_global_device_ids=true | all-gather | bytes 680 | tf_op jit(solution)/shard_map/all_gather | solution.py:13
  62.7 0.6 copy.48
  63.3 0.5 broadcast.65
  63.8 0.6 reduce.2
  64.4 0.1 reshape.150
  64.5 0.1 fusion.20
  64.6 18.2 %all_gather.20 = bf16[16,20,56]{2,1,0:T(8,128)(2,1)S(1)} all-gather(bf16[1,20,56]{2,1,0:T(8,128)(2,1)S(1)} %fusion.20), channel_id=1, replica_groups=mesh['grp'=16,'span'=2] {'grp'}, dimensions={0}, use_global_device_ids=true | all-gather | bytes 38080 | tf_op jit(solution)/shard_map/all_gather | solution.py:13
  82.8 5.6 %all-gather.5.cloned.1.call-done = bf16[16,20,56,112]{3,2,1,0:T(8,128)(2,1)} async-done(((bf16[1,20,56,112]{3,2,1,0:T(8,128)(2,1)}), bf16[16,20,56,112]{3,2,1,0:T(8,128)(2,1)}) %all-gather.5.cloned.1.call-update) | async-done | bytes 4014096 | tf_op jit(solution)/shard_map/all_gather | solution.py:13
  88.4 1.9 while.14
  88.4 0.7 fusion.40
  89.1 0.1 convert_add_fusion.5
  89.2 1.1 convert_add_fusion.4
  90.4 0.8 convert_bitcast_fusion.3
  91.2 0.7 reshape.151
  91.9 3.2 %all-to-all-start.4 = ((bf16[2,2,560]{2,1,0:T(2,128)(2,1)}), bf16[2,2,560]{2,1,0:T(2,128)(2,1)S(1)}, u32[]{:S(2)}, u32[]{:S(2)}) async-start(bf16[2,2,560]{2,1,0:T(2,128)(2,1)} %reshape.151), calls=%async_computation.4 | async-start | bytes 10240 | tf_op jit(solution)/shard_map/all_to_all | solution.py:101
  95.1 0.8 convert_bitcast_fusion.1
  95.8 0.9 pad_maximum_fusion.2
  96.8 0.9 all-to-all-done.4
  97.7 3.5 %all-to-all-start.3 = ((bf16[2,20,56,112]{3,2,1,0:T(8,128)(2,1)}), bf16[2,20,56,112]{3,2,1,0:T(8,128)(2,1)S(1)}, u32[]{:S(2)}, u32[]{:S(2)}) async-start(bf16[2,20,56,112]{3,2,1,0:T(8,128)(2,1)} %pad_maximum_fusion.2), calls=%async_computation.3 | async-start | bytes 1146880 | tf_op jit(solution)/shard_map/all_to_all | solution.py:98
  101.2 0.0 all-gather.7.cloned.1.call-start
  101.3 0.1 reshape.152
  101.4 0.1 reshape.140
  101.5 0.1 add_bitcast_fusion
  101.6 0.6 fusion.24
  102.1 8.1 %all-to-all-done.3 = bf16[2,20,56,112]{3,2,1,0:T(8,128)(2,1)S(1)} async-done(((bf16[2,20,56,112]{3,2,1,0:T(8,128)(2,1)}), bf16[2,20,56,112]{3,2,1,0:T(8,128)(2,1)S(1)}, u32[]{:S(2)}, u32[]{:S(2)}) %all-to-all-start.3) | async-done | bytes 501792 | tf_op jit(solution)/shard_map/all_to_all | solution.py:98
  110.2 0.1 convert_bitcast_fusion
  110.3 0.1 copy.25
  110.3 0.2 fusion.15
  110.6 1.1 multiply_reduce_fusion
  111.7 0.9 fusion.14
  112.6 0.2 reshape.141
  112.8 84.7 %all-gather.9.cloned.1.call-done = bf16[2240,2,1536]{2,1,0:T(2,128)(2,1)} async-done(((bf16[140,2,1536]{2,1,0:T(2,128)(2,1)}), bf16[2240,2,1536]{2,1,0:T(2,128)(2,1)}) %all-gather.9.cloned.1.call-update) | async-done | bytes 13762576 | tf_op jit(solution)/shard_map/all_gather | solution.py:116
  197.5 14.4 %copy.35 = bf16[280,8,2,1536]{3,1,2,0:T(8,128)(2,1)} copy(bf16[280,8,2,1536]{3,2,1,0:T(2,128)(2,1)} %bitcast.147) | data formatting | bytes 27525120
  211.8 7.3 %all-gather.7.cloned.1.call-done = bf16[256,2240]{0,1:T(8,128)(2,1)} async-done(((bf16[128,2240]{0,1:T(8,128)(2,1)}), bf16[256,2240]{0,1:T(8,128)(2,1)}) %all-gather.7.cloned.1.call-update) | async-done | bytes 1146896 | tf_op jit(solution)/shard_map/all_gather | solution.py:119
  219.2 9.2 %convolution_convert_fusion = bf16[256,3072]{1,0:T(8,128)(2,1)S(1)} fusion(bf16[256,2240]{0,1:T(8,128)(2,1)} %all-gather.7.cloned.1.call-done, bf16[2240,3072]{1,0:T(8,128)(2,1)} %bitcast.144), kind=kOutput, calls=%fused_computation.17 | convolution fusion | flops 3524001792 | bytes 16482304 | tf_op jit(solution)/shard_map/dot_general | solution.py:118
  228.4 1.3 fusion.28
  229.6 2.6 collective-permute-start.1
  232.2 3.2 %collective-permute-start = (bf16[1,8,16,3072]{3,2,1,0:T(8,128)(2,1)}, bf16[1,8,16,3072]{3,2,1,0:T(8,128)(2,1)}, u32[]{:S(2)}, u32[]{:S(2)}) collective-permute-start(bf16[1,8,16,3072]{3,2,1,0:T(8,128)(2,1)} %bitcast.27), channel_id=1, source_target_pairs={{0,2},{2,4},{4,6},{6,8},{8,10},{10,12},{12,14},{14,16},{16,18},{18... | collective-permute-start | bytes 2359304 | tf_op jit(solution)/shard_map/ppermute | solution.py:47
  235.4 0.1 fusion.30
  235.5 0.2 fusion.29
  235.7 7.5 %collective-permute-done.1 = bf16[1,8,16,3072]{3,2,1,0:T(8,128)(2,1)S(1)} collective-permute-done((bf16[1,8,16,3072]{3,2,1,0:T(8,128)(2,1)}, bf16[1,8,16,3072]{3,2,1,0:T(8,128)(2,1)S(1)}, u32[]{:S(2)}, u32[]{:S(2)}) %collective-permute-start.1) | collective-permute-done | bytes 786464 | tf_op jit(solution)/shard_map/ppermute | solution.py:48
  243.1 8.7 %collective-permute-done = bf16[1,8,16,3072]{3,2,1,0:T(8,128)(2,1)} collective-permute-done((bf16[1,8,16,3072]{3,2,1,0:T(8,128)(2,1)}, bf16[1,8,16,3072]{3,2,1,0:T(8,128)(2,1)}, u32[]{:S(2)}, u32[]{:S(2)}) %collective-permute-start) | collective-permute-done | bytes 786464 | tf_op jit(solution)/shard_map/ppermute | solution.py:47
  251.8 3.5 %select_maximum_fusion = bf16[4,10,18,3072]{3,2,1,0:T(8,128)(2,1)S(1)} fusion(bf16[1,8,16,3072]{3,2,1,0:T(8,128)(2,1)S(1)} %collective-permute-done.1, bf16[2,8,16,3072]{3,2,1,0:T(8,128)(2,1)S(1)} %bitcast.145, bf16[1,8,16,3072]{3,2,1,0:T(8,128)(2,1)} %collective-permute-done), kind=kLoop, calls=%fused_computation.12 | loop fusion | flops 42024960 | bytes 7569408 | tf_op jit(solution)/shard_map/concatenate | solution.py:49
  255.3 13.7 %multiply_add_fusion = f32[2,8,16,3072]{3,2,1,0:T(8,128)} fusion(bf16[2,8,16,3072]{3,2,1,0:T(8,128)(2,1)S(1)} %bitcast.146, bf16[4,10,18,3072]{3,2,1,0:T(8,128)(2,1)S(1)} %select_maximum_fusion, bf16[1,8,16,3072]{3,2,1,0:T(8,128)(2,1)S(1)} %collective-permute-done.1, bf16[1,8,16,3072]{3,2,1,0:T(8,128)(2,1)} %collective-permute-done, f32[3072]{0:T(1024)S(1)} %bitcast.163, ...), kind=kLoop, calls=%fused_computation.18 | loop fusion | flops 65273856 | bytes 44384256 | tf_op jit(solution)/shard_map/add | solution.py:136
  269.1 5.6 %reshape.133 = f32[256,2,1536]{2,1,0:T(2,128)} reshape(f32[2,8,16,3072]{3,2,1,0:T(8,128)} %multiply_add_fusion) | data formatting | bytes 6291456 | tf_op jit(solution)/shard_map/reshape | solution.py:139
  274.7 5.6 %fusion.27 = (f32[256,1,1536]{2,1,0:T(1,128)S(1)}, f32[256,1,1536]{2,1,0:T(1,128)S(1)}) fusion(f32[256,2,1536]{2,1,0:T(2,128)} %reshape.133), kind=kLoop, calls=%fused_computation.69 | loop fusion | bytes 6291456 | tf_op jit(solution)/shard_map/slice | solution.py:140
  280.3 1.3 fusion.9
  (31 shorter events, 0.3 us)
Async XLA Ops:
  6.5 5.7 %copy-start = (bf16[128,2240]{0,1:T(8,128)(2,1)S(1)}, bf16[128,2240]{0,1:T(8,128)(2,1)}, u32[]{:S(2)}) copy-start(bf16[128,2240]{0,1:T(8,128)(2,1)} %param.11) | copy-start | bytes 1720324
  7.8 6.3 %all-to-all-start = ((f32[2,1,20]{2,1,0:T(1,128)}), f32[2,1,20]{2,1,0:T(1,128)S(1)}, u32[]{:S(2)}, u32[]{:S(2)}) async-start(f32[2,1,20]{2,1,0:T(1,128)} %broadcast_in_dim.19), calls=%async_computation | async-start | bytes 2048 | tf_op jit(solution)/shard_map/all_to_all | solution.py:84
  12.7 20.0 %copy-start.2 = (bf16[128,2240]{0,1:T(8,128)(2,1)S(1)}, bf16[128,2240]{0,1:T(8,128)(2,1)}, u32[]{:S(2)}) copy-start(bf16[128,2240]{0,1:T(8,128)(2,1)} %param.10) | copy-start | bytes 1720324
  14.1 17.0 %all-to-all-start.1 = ((f32[2,20,56,112]{3,2,1,0:T(8,128)}), f32[2,20,56,112]{3,2,1,0:T(8,128)S(1)}, u32[]{:S(2)}, u32[]{:S(2)}) async-start(f32[2,20,56,112]{3,2,1,0:T(8,128)} %bitcast.149), calls=%async_computation.1 | async-start | bytes 2293760 | tf_op jit(solution)/shard_map/all_to_all | solution.py:85
  17.7 70.6 %all-gather.5.cloned.1.call-start = ((), (), s32[]{:S(2)}) async-start(), calls=%async_computation.5 | async-start | bytes 4874240 | tf_op jit(solution)/shard_map/all_gather | solution.py:13
  32.0 165.5 %all-gather.9.cloned.1.call-start = ((), (), s32[]{:S(2)}) async-start(), calls=%async_computation.7 | async-start | bytes 14622720 | tf_op jit(solution)/shard_map/all_gather | solution.py:116
  33.8 29.5 %all-to-all-start.2 = ((f32[2,1,1120]{2,1,0:T(1,128)}), f32[2,1,1120]{2,1,0:T(1,128)S(1)}, u32[]{:S(2)}, u32[]{:S(2)}) async-start(f32[2,1,1120]{2,1,0:T(1,128)} %reshape.149), calls=%async_computation.2 | async-start | bytes 18432 | tf_op jit(solution)/shard_map/all_to_all | solution.py:86
  64.5 23.8 %copy-start.4 = (f32[2,20,56]{2,1,0:T(8,128)}, f32[2,20,56]{2,1,0:T(8,128)S(1)}, u32[]{:S(2)}) copy-start(f32[2,20,56]{2,1,0:T(8,128)S(1)} %reshape.150) | copy-start | bytes 26884
  90.3 11.1 %copy-start.5 = (f32[20,112]{1,0:T(8,128)S(1)}, f32[20,112]{1,0:T(8,128)}, u32[]{:S(2)}) copy-start(f32[20,112]{1,0:T(8,128)} %reduce_sum.21) | copy-start | bytes 26884
  90.3 11.1 %copy-start.7 = (f32[1,20]{1,0:T(1,128)S(1)}, f32[1,20]{1,0:T(1,128)}, u32[]{:S(2)}) copy-start(f32[1,20]{1,0:T(1,128)} %param.12) | copy-start | bytes 244
  91.9 5.9 %all-to-all-start.4 = ((bf16[2,2,560]{2,1,0:T(2,128)(2,1)}), bf16[2,2,560]{2,1,0:T(2,128)(2,1)S(1)}, u32[]{:S(2)}, u32[]{:S(2)}) async-start(bf16[2,2,560]{2,1,0:T(2,128)(2,1)} %reshape.151), calls=%async_computation.4 | async-start | bytes 10240 | tf_op jit(solution)/shard_map/all_to_all | solution.py:101
  97.7 12.5 %all-to-all-start.3 = ((bf16[2,20,56,112]{3,2,1,0:T(8,128)(2,1)}), bf16[2,20,56,112]{3,2,1,0:T(8,128)(2,1)S(1)}, u32[]{:S(2)}, u32[]{:S(2)}) async-start(bf16[2,20,56,112]{3,2,1,0:T(8,128)(2,1)} %pad_maximum_fusion.2), calls=%async_computation.3 | async-start | bytes 1146880 | tf_op jit(solution)/shard_map/all_to_all | solution.py:98
  101.2 118.0 %all-gather.7.cloned.1.call-start = ((), (), s32[]{:S(2)}) async-start(), calls=%async_computation.6 | async-start | bytes 1720320 | tf_op jit(solution)/shard_map/all_gather | solution.py:119
  110.5 2.0 copy-start.3
  228.3 7.1 %copy-start.6 = (f32[2,1536]{1,0:T(2,128)S(1)}, f32[2,1536]{1,0:T(2,128)}, u32[]{:S(2)}) copy-start(f32[2,1536]{1,0:T(2,128)} %param.15) | copy-start | bytes 36868
  229.6 13.5 %collective-permute-start.1 = (bf16[1,8,16,3072]{3,2,1,0:T(8,128)(2,1)}, bf16[1,8,16,3072]{3,2,1,0:T(8,128)(2,1)S(1)}, u32[]{:S(2)}, u32[]{:S(2)}) collective-permute-start(bf16[1,8,16,3072]{3,2,1,0:T(8,128)(2,1)} %bitcast.29), channel_id=1, source_target_pairs={{2,0},{4,2},{6,4},{8,6},{10,8},{12,10},{14,12},{16,14},{18,16},{20... | collective-permute-start | bytes 2359304 | tf_op jit(solution)/shard_map/ppermute | solution.py:48
  232.2 19.6 %collective-permute-start = (bf16[1,8,16,3072]{3,2,1,0:T(8,128)(2,1)}, bf16[1,8,16,3072]{3,2,1,0:T(8,128)(2,1)}, u32[]{:S(2)}, u32[]{:S(2)}) collective-permute-start(bf16[1,8,16,3072]{3,2,1,0:T(8,128)(2,1)} %bitcast.27), channel_id=1, source_target_pairs={{0,2},{2,4},{4,6},{6,8},{8,10},{10,12},{12,14},{14,16},{16,18},{18... | collective-permute-start | bytes 2359304 | tf_op jit(solution)/shard_map/ppermute | solution.py:47
  274.7 6.9 %copy-start.1 = (bf16[128,2240]{0,1:T(8,128)(2,1)S(1)}, bf16[128,2240]{0,1:T(8,128)(2,1)}, u32[]{:S(2)}) copy-start(bf16[128,2240]{0,1:T(8,128)(2,1)} %param.11) | copy-start | bytes 1720324
Sparse Core Ops, SparseCore 0:
  32.1 56.1 all-gather.4
  90.6 106.7 all-gather.8
  199.0 20.1 all-gather.6
where the time goes:
time: 290 us; the launch traced here: 288 us
  waiting for transfers between devices  137 us (47%)
  blocking collectives  42.1 us (15%)
  local copies, waits for them, and re-layouts  33.3 us (11%)
  other arithmetic  28.7 us (10%)
  starting transfers between devices  22.7 us (8%)
  between operations  13.4 us (5%)
  matrix products  11.3 us (4%)
    all_gather x1, waiting for transfers between devices, shards(): full_weight = lax.all_gather(up_weight, 'grp', axis=0, tiled=True)  84.7 us
    all_gather x2, blocking collectives, prefix_2(): lax.all_gather(a.astype(kind), axis)  42.1 us
    unnamed x22, local copies, waits for them, and re-layouts  16.6 us
    add x1, other arithmetic, shards(): mixed + visible_extent.astype(jnp.float32) * convolution_kernel[tap_t, ta...  13.7 us
    all_to_all x1, waiting for transfers between devices, shards(): lax.all_to_all(outgoing_memory, 'span', split_axis=0, concat_axis=0, tile...  12.8 us
    dot_general x1, matrix products, shards(): jnp.dot(lax.all_gather(normed, 'span', axis=0, tiled=True), flat_weight,...  9.16 us
    ppermute x1, waiting for transfers between devices, extended_2(): before = lax.ppermute(last, axis, up)  8.7 us
    all_to_all x1, waiting for transfers between devices, shards(): lax.all_to_all(as_sent(stack_state), 'span', split_axis=0, concat_axis=0,...  8.06 us
  transfers between devices with their start and end apart: 10, of which 9 were waited for; matrix products, arithmetic and copies ran while one was open for 11% of the time, Pallas kernels for 0%

commit v1 on v0

v1 whole, which is shorter than its diff:
```python
import functools

import jax
import jax.numpy as jnp
from jax import lax
from jax.experimental import pallas as pl
from jax.experimental.pallas import tpu as pltpu
from jax.sharding import PartitionSpec as P

FH = 8
FW = 16
BLOCK = 8
MESH = pl.DeviceIdType.MESH


def swap(x, groups):
    return lax.ppermute(x, "grp", [(i, i ^ 1) for i in range(groups)])


def fused(groups, members, heads, head_dim, kt_ref, v_ref, q_ref, ret_ref, w_ref, wg_ref, nrm_ref,
          local, outbox, inbox, tot_out, tot_in, back_out, back_in, within, attend, normed,
          s1, r1, s2, r2, s3, r3, sw, rw, sx, rx, sn, rn, sc, rc, lsem):
    grp = lax.axis_index("grp")
    span = lax.axis_index("span")
    me = grp * members + span
    spot = me % BLOCK
    layer = me // BLOCK
    layers = groups * members // BLOCK
    core = grp % 2
    chip = grp // 2
    chips = groups // 2
    rows = heads * head_dim // BLOCK

    def device(r):
        return (r // members, r % members)

    even = chip % 2 == 0
    place = jnp.where(even, chip // 2, chips - 1 - chip // 2)

    def chip_at(p):
        p = (p + chips) % chips
        return jnp.where(p < chips // 2, 2 * p, 2 * (chips - 1 - p) + 1)

    right = (2 * chip_at(place + 1) + core, span)
    left = (2 * chip_at(place - 1) + core, span)
    twin = (2 * chip + 1 - core, span)
    mates = [(spot + k) % BLOCK for k in range(1, BLOCK)]
    others = [(layer + k) % layers for k in range(1, layers)]

    barrier = pltpu.get_barrier_semaphore()
    targets = [device(layer * BLOCK + m) for m in mates]
    targets += [device(o * BLOCK + spot) for o in others]
    targets += [right, left, twin]
    for t in targets:
        pl.semaphore_signal(barrier, inc=1, device_id=t, device_id_type=MESH)
    pl.semaphore_wait(barrier, len(targets))

    def send(src, dst, ssem, rsem, to):
        return pltpu.make_async_remote_copy(
            src_ref=src, dst_ref=dst, send_sem=ssem, recv_sem=rsem, device_id=to, device_id_type=MESH
        )

    across = send(w_ref.at[1 - core], wg_ref.at[chip, core], sx, rx, twin)
    across.start()
    keep = pltpu.make_async_copy(w_ref.at[core], wg_ref.at[chip, core], lsem.at[0])
    keep.start()

    half = chips // 2

    def halves(way, hop):
        if hop == half - 1:
            return (way,)
        return (0, 1)

    def hop_copy(way, hop, part):
        source = chip_at(place - hop) if way == 0 else chip_at(place + hop)
        at = wg_ref.at[source, part]
        return send(at, at, sw.at[way, hop, part], rw.at[way, hop, part], right if way == 0 else left)

    def hop_wait(way, hop, part):
        source = chip_at(place - hop - 1) if way == 0 else chip_at(place + hop + 1)
        at = wg_ref.at[source, part]
        send(at, at, sw.at[way, hop, part], rw.at[way, hop, part], right if way == 0 else left).wait_recv()

    started = []

    def ring(hop):
        for way in (0, 1):
            if hop == 0:
                continue
            for part in halves(way, hop - 1):
                hop_wait(way, hop - 1, part)
        if hop < half:
            for way in (0, 1):
                for part in halves(way, hop):
                    c = hop_copy(way, hop, part)
                    c.start()
                    started.append(c)

    lane = lax.broadcasted_iota(jnp.int32, (head_dim, 128), 1)
    for h in range(heads):
        state = jnp.dot(kt_ref[h], v_ref[h], preferred_element_type=jnp.float32)
        keepf = jnp.full((head_dim, 128), ret_ref[0, h], jnp.float32)
        high = keepf.astype(jnp.bfloat16).astype(jnp.float32)
        state = jnp.where(lane == head_dim + 1, high, state)
        state = jnp.where(lane == head_dim + 2, keepf - high, state)
        local[h * head_dim : (h + 1) * head_dim, :] = state
    for j in range(BLOCK):
        outbox[j] = local[j * rows : (j + 1) * rows, :].astype(jnp.bfloat16)
    pltpu.make_async_copy(outbox.at[spot], inbox.at[spot], lsem.at[1]).start()
    first = [
        send(outbox.at[m], inbox.at[spot], s1.at[m], r1.at[spot], device(layer * BLOCK + m)) for m in mates
    ]
    for c in first:
        c.start()

    keep.wait()
    across.wait()
    ring(0)

    pltpu.make_async_copy(outbox.at[spot], inbox.at[spot], lsem.at[1]).wait()
    for m in mates:
        send(outbox.at[m], inbox.at[m], s1.at[m], r1.at[m], device(layer * BLOCK + m)).wait_recv()
    wide = lax.broadcasted_iota(jnp.int32, (rows, 128), 1)

    def factor_of(x):
        return x[:, head_dim + 1 : head_dim + 2] + x[:, head_dim + 2 : head_dim + 3]

    running = jnp.zeros((rows, 128), jnp.float32)
    factor = jnp.ones((rows, 1), jnp.float32)
    factors = []
    for j in range(BLOCK):
        within[j] = running
        factors.append(factor)
        got = inbox[j].astype(jnp.float32)
        f = factor_of(got)
        running = f * running + got
        factor = factor * f
    full = jnp.broadcast_to(factor, (rows, 128))
    high = full.astype(jnp.bfloat16).astype(jnp.float32)
    total = jnp.where(wide == head_dim + 1, high, running)
    total = jnp.where(wide == head_dim + 2, full - high, total)
    tot_out[...] = total.astype(jnp.bfloat16)
    second = [
        send(tot_out, tot_in.at[layer], s2.at[o], r2.at[layer], device(o * BLOCK + spot)) for o in others
    ]
    for c in second:
        c.start()
    for o in others:
        send(tot_out, tot_in.at[o], s2.at[o], r2.at[o], device(o * BLOCK + spot)).wait_recv()

    def earlier(i, carry):
        got = tot_in[i].astype(jnp.float32)
        return factor_of(got) * carry + got

    before = lax.fori_loop(0, layer, earlier, jnp.zeros((rows, 128), jnp.float32))
    for j in range(BLOCK):
        back_out[j] = (factors[j] * before + within[j]).astype(jnp.bfloat16)
    pltpu.make_async_copy(back_out.at[spot], back_in.at[spot], lsem.at[2]).start()
    third = [
        send(back_out.at[m], back_in.at[spot], s3.at[m], r3.at[spot], device(layer * BLOCK + m)) for m in mates
    ]
    for c in third:
        c.start()
    pltpu.make_async_copy(back_out.at[spot], back_in.at[spot], lsem.at[2]).wait()
    for m in mates:
        send(back_out.at[m], back_in.at[m], s3.at[m], r3.at[m], device(layer * BLOCK + m)).wait_recv()
    for j in range(BLOCK):
        part = slice(j * rows, (j + 1) * rows)
        got = local[part, :]
        local[part, :] = factor_of(got) * back_in[j].astype(jnp.float32) + got

    squares = jnp.zeros((128, 1), jnp.float32)
    column = lax.broadcasted_iota(jnp.int32, (q_ref.shape[1], 128), 1)
    for h in range(heads):
        state = local[h * head_dim : (h + 1) * head_dim, :].astype(jnp.bfloat16)
        numer = jnp.dot(q_ref[h], state, preferred_element_type=jnp.float32)
        value = numer / (numer[:, head_dim : head_dim + 1] + 0.0001)
        value = jnp.where(column < head_dim, value, 0.0)
        squares = squares + jnp.sum(value * value, axis=1, keepdims=True)
        attend[h] = value
    scale = lax.rsqrt(squares / (heads * head_dim) + 1e-06)
    for h in range(heads):
        normed[h] = (attend[h] * scale).astype(jnp.bfloat16)
    keepn = pltpu.make_async_copy(normed, nrm_ref.at[core, span], lsem.at[3])
    keepn.start()
    peers = [(span + k) % members for k in range(1, members)]
    fourth = [
        send(normed, nrm_ref.at[core, span], sn.at[p], rn.at[span], (grp, p)) for p in peers
    ]
    for c in fourth:
        c.start()
    cross = [send(normed, nrm_ref.at[core, span], sc.at[span], rc.at[span], twin)]
    cross[0].start()
    ring(1)
    for p in peers:
        send(normed, nrm_ref.at[core, p], sn.at[p], rn.at[p], (grp, p)).wait_recv()
        c = send(nrm_ref.at[core, p], nrm_ref.at[core, p], sc.at[p], rc.at[p], twin)
        c.start()
        cross.append(c)
    for hop in range(2, half + 1):
        ring(hop)
    keepn.wait()
    for p in [span] + peers:
        send(nrm_ref.at[1 - core, p], nrm_ref.at[1 - core, p], sc.at[p], rc.at[p], twin).wait_recv()
    for c in first + second + third + fourth + cross + started:
        c.wait_send()


def gather_and_attend(queries, key_rows, value_rows, retention, up_weight):
    groups = lax.axis_size("grp")
    members = lax.axis_size("span")
    tokens, dim = queries.shape
    heads = retention.shape[1]
    head_dim = dim // heads
    rows, _, width = up_weight.shape
    part = width // 2
    depth = -(-rows // 16) * 16
    kt = jnp.maximum(key_rows, 0).T.reshape(heads, head_dim, tokens)
    q = jnp.maximum(queries, 0).reshape(tokens, heads, head_dim).transpose(1, 0, 2)
    v = value_rows.reshape(tokens, heads, head_dim).transpose(1, 0, 2)
    rest = 128 - head_dim
    one = jnp.ones((heads, tokens, 1), v.dtype)
    v = jnp.concatenate([v, one, jnp.zeros((heads, tokens, rest - 1), v.dtype)], axis=2)
    w = up_weight.reshape(rows, 2, 2, part).transpose(2, 0, 1, 3).reshape(2, rows, width)
    w = jnp.pad(w, ((0, 0), (0, depth - rows), (0, 0)))
    chips = groups // 2
    share = dim // BLOCK
    layers = groups * members // BLOCK
    dma = pltpu.SemaphoreType.DMA
    vmem = pl.BlockSpec(memory_space=pltpu.VMEM)
    anywhere = pl.BlockSpec(memory_space=pl.ANY)
    bf = jnp.bfloat16
    slabs = pltpu.VMEM((BLOCK, share, 128), bf)
    weight, normed = pl.pallas_call(
        functools.partial(fused, groups, members, heads, head_dim),
        out_shape=(
            jax.ShapeDtypeStruct((chips, 2, depth, width), bf),
            jax.ShapeDtypeStruct((2, members, heads, tokens, 128), bf),
        ),
        in_specs=[vmem, vmem, vmem, pl.BlockSpec(memory_space=pltpu.SMEM), anywhere],
        out_specs=(anywhere, anywhere),
        scratch_shapes=[
            pltpu.VMEM((dim, 128), jnp.float32),
            slabs,
            slabs,
            pltpu.VMEM((share, 128), bf),
            pltpu.VMEM((layers, share, 128), bf),
            slabs,
            slabs,
            pltpu.VMEM((BLOCK, share, 128), jnp.float32),
            pltpu.VMEM((heads, tokens, 128), jnp.float32),
            pltpu.VMEM((heads, tokens, 128), bf),
            dma((BLOCK,)), dma((BLOCK,)),
            dma((layers,)), dma((layers,)),
            dma((BLOCK,)), dma((BLOCK,)),
            dma((2, chips // 2, 2)), dma((2, chips // 2, 2)),
            dma, dma,
            dma((members,)), dma((members,)),
            dma((members,)), dma((members,)),
            dma((4,)),
        ],
        compiler_params=pltpu.CompilerParams(
            collective_id=0, has_side_effects=True, vmem_limit_bytes=32 * 1024 * 1024
        ),
        name="gather_and_attend",
    )(kt, v, q, retention, w)
    weight = weight.reshape(groups * depth, width)
    normed = normed.reshape(2 * members, heads, tokens, 128)[..., :head_dim]
    normed = normed.transpose(0, 2, 1, 3).reshape(2 * members * tokens, groups, rows)
    normed = jnp.pad(normed, ((0, 0), (0, 0), (0, depth - rows)))
    return normed.reshape(2 * members * tokens, groups * depth), weight


def shards(queries, key_rows, value_rows, retention, up_weight, conv_weight, conv_bias):
    normed, flat_weight = gather_and_attend(queries, key_rows, value_rows, retention, up_weight)
    groups = lax.axis_size("grp")
    core = lax.axis_index("grp") % 2
    up_vals = jnp.dot(normed, flat_weight, preferred_element_type=jnp.float32)
    up_vals = up_vals.astype(jnp.bfloat16)
    part = flat_weight.shape[1] // 2
    frames = up_vals.shape[0] // (FH * FW)
    grid = up_vals.reshape(frames, FH, FW, 2 * part)
    onward = [(i, i + 2) for i in range(groups - 2)]
    before = lax.ppermute(grid[-1:], "grp", onward)
    after = lax.ppermute(grid[:1], "grp", [(j, i) for i, j in onward])
    extended = jnp.concatenate([before, grid, after], axis=0)
    padded = jnp.pad(extended, ((0, 0), (1, 1), (1, 1), (0, 0)))
    taps = lax.dynamic_slice_in_dim(conv_weight, core * part, part, axis=4)
    convolution_kernel = taps.reshape(3, 3, 3, 2 * part).astype(jnp.float32)
    bias = lax.dynamic_slice_in_dim(conv_bias, core * part, part, axis=1)
    mixed = jnp.zeros((frames, FH, FW, 2 * part), jnp.float32) + bias.reshape(2 * part)
    for tap_t in range(3):
        for tap_y in range(3):
            for tap_x in range(3):
                visible_extent = padded[
                    tap_t : tap_t + frames, tap_y : tap_y + FH, tap_x : tap_x + FW
                ]
                mixed = (
                    mixed
                    + visible_extent.astype(jnp.float32) * convolution_kernel[tap_t, tap_y, tap_x]
                )
    mixed = mixed.reshape(2, frames * FH * FW // 2, 2, part)
    hidden = (mixed[:, :, 0] * jax.nn.silu(mixed[:, :, 1])).astype(jnp.bfloat16)
    mine = lax.dynamic_index_in_dim(hidden, core, 0, False)
    theirs = swap(lax.dynamic_index_in_dim(hidden, 1 - core, 0, False), groups)
    first = jnp.where(core == 0, mine, theirs)
    second = jnp.where(core == 0, theirs, mine)
    return jnp.concatenate([first, second], axis=1)


def solution(mesh):
    in_specs = (
        P(("grp", "span"), None),
        P(("grp", "span"), None),
        P(("grp", "span"), None),
        P(("grp", "span"), None),
        P("grp", None, "span"),
        P(None, None, None, None, "span"),
        P(None, "span"),
    )
    out_specs = P("grp", "span")
    return jax.shard_map(shards, mesh=mesh, in_specs=in_specs, out_specs=out_specs, check_vma=False)
```

time: 290 us -> 172 us (0.59)
  the two profiles are of different devices: /device:TPU:1 before, /device:TPU:7 now
where the time goes in v1:
time: 172 us
  Pallas kernels  97.5 us (57%)
  local copies, waits for them, and re-layouts  24.8 us (14%)
  other arithmetic  19.3 us (11%)
  waiting for transfers between devices  15.9 us (9%)
  matrix products  6.97 us (4%)
  starting transfers between devices  6.92 us (4%)
    pallas_call x1, Pallas kernels, gather_and_attend(): pl.pallas_call(functools.partial(fused, groups, members, heads, head_dim)...  97.5 us
    add x1, other arithmetic, shards(): mixed + visible_extent.astype(jnp.float32) * convolution_kernel[tap_t, ta...  12.9 us
    ppermute x1, waiting for transfers between devices, shards(): before = lax.ppermute(grid[-1:], 'grp', onward)  9.53 us
    unnamed x17, local copies, waits for them, and re-layouts  7.29 us
    dot_general x1, matrix products, shards(): up_vals = jnp.dot(normed, flat_weight, preferred_element_type=jnp.float32)  6.97 us
    slice x1, local copies, waits for them, and re-layouts, shards(): hidden = (mixed[:, :, 0] * jax.nn.silu(mixed[:, :, 1])).astype(jnp.bfloat16)  5.68 us
    ppermute x1, waiting for transfers between devices, shards(): after = lax.ppermute(grid[:1], 'grp', [(j, i) for i, j in onward])  4.99 us
  transfers between devices with their start and end apart: 3, of which 3 were waited for; matrix products, arithmetic and copies ran while one was open for 1% of the time, Pallas kernels for 0%

profile of v1, /device:TPU:7, one launch (start us, length us, event | category | flops | bytes accessed | tf_op | source)
XLA Modules:
  0.0 171.7 jit_solution(10795556798277035959)
XLA Ops:
  0.0 0.0 copy-start
  0.0 1.9 %broadcast_maximum_fusion.1 = bf16[128,2240]{0,1:T(8,128)(2,1)} fusion(bf16[128,2240]{0,1:T(8,128)(2,1)} %param.8), kind=kLoop, calls=%fused_computation.27 | loop fusion | flops 286720 | bytes 1146880 | tf_op jit(solution)/shard_map/max | solution.py:219
  1.9 1.4 copy.11
  3.3 0.1 pad.26.clone
  3.4 0.1 pad.25.clone
  3.5 1.1 broadcast_maximum_fusion
  4.6 0.3 copy.12
  4.9 0.0 copy-start.2
  4.9 1.8 %copy.30 = bf16[140,1,2,2,768]{4,3,1,0,2:T(2,128)(2,1)S(1)} copy(bf16[140,1,2,2,768]{4,3,2,1,0:T(2,128)(2,1)} %bitcast.55) | data formatting | bytes 1720320 | tf_op jit(solution)/shard_map/reshape | solution.py:225
  6.7 0.5 reshape.43
  7.2 0.1 pad.12.w_ref
  7.3 0.2 maximum_maximum_fusion.v_ref
  7.6 0.0 copy-done.2
  7.6 0.0 copy-start.1
  7.6 1.1 copy-done.1
  8.6 97.5 %gather_and_attend.1 = (bf16[8,2,144,1536]{3,2,1,0:T(8,128)(2,1)S(1)}, bf16[2,2,20,128,128]{4,3,2,1,0:T(8,128)(2,1)S(1)}) custom-call(bf16[20,112,128]{2,1,0:T(8,128)(2,1)S(1)} %bitcast.46, bf16[20,128,128]{2,1,0:T(8,128)(2,1)S(1)} %maximum_maximum_fusion.v_ref, bf16[20,128,112]{2,1,0:T(8,128)(2,1)S(1)} %bitcast.45, f32[1,20]{1,0:T(1,128)S(1)} %copy-done.2, ...), custom_call_target="tpu_custom_call" | custom-call | tf_op jit(solution)/shard_map/gather_and_attend/pallas_call | solution.py:235
  106.1 0.0 copy-start.3
  106.1 2.9 %copy-done.3 = bf16[8,2,144,1536]{3,2,1,0:T(8,128)(2,1)} copy-done((bf16[8,2,144,1536]{3,2,1,0:T(8,128)(2,1)}, bf16[8,2,144,1536]{3,2,1,0:T(8,128)(2,1)S(1)}, u32[]{:S(2)}) %copy-start.3) | copy-done | bytes 7077912
  109.0 3.3 %copy.17 = bf16[4,20,128,112]{2,0,3,1:T(4,128)(2,1)} copy(bf16[4,20,128,112]{3,2,1,0:T(8,128)(2,1)S(1)} %bitcast.44) | data formatting | bytes 4587520
  112.3 2.8 %reshape.45 = bf16[512,16,140]{0,2,1:T(8,128)(2,1)S(1)} reshape(bf16[4,128,20,112]{1,0,3,2:T(4,128)(2,1)} %bitcast.50) | data formatting | bytes 4587520 | tf_op jit(solution)/shard_map/reshape | solution.py:270
  115.2 0.2 pad.13
  115.4 0.0 copy-start.6
  115.4 7.0 %convolution_convert_fusion = bf16[512,1536]{1,0:T(8,128)(2,1)S(1)} fusion(bf16[512,2304]{0,1:T(8,128)(2,1)S(1)} %bitcast.53, bf16[2304,1536]{1,0:T(8,128)(2,1)} %bitcast.47), kind=kOutput, calls=%fused_computation.13 | convolution fusion | flops 3624665088 | bytes 11010048 | tf_op jit(solution)/shard_map/dot_general | solution.py:279
  122.4 0.0 copy-start.4
  122.4 0.1 fusion.9
  122.5 3.4 %collective-permute-start.1 = (bf16[1,8,16,1536]{3,2,1,0:T(8,128)(2,1)S(1)}, bf16[1,8,16,1536]{3,2,1,0:T(8,128)(2,1)S(1)}, u32[]{:S(2)}, u32[]{:S(2)}) collective-permute-start(bf16[1,8,16,1536]{3,2,1,0:T(8,128)(2,1)S(1)} %bitcast.58), channel_id=1, source_target_pairs={{4,0},{6,2},{8,4},{10,6},{12,8},{14,10},{16,12},{18,14},{20,16},{2... | collective-permute-start | bytes 1179656 | tf_op jit(solution)/shard_map/ppermute | solution.py:286
  125.9 3.0 %collective-permute-start = (bf16[1,8,16,1536]{3,2,1,0:T(8,128)(2,1)S(1)}, bf16[1,8,16,1536]{3,2,1,0:T(8,128)(2,1)S(1)}, u32[]{:S(2)}, u32[]{:S(2)}) collective-permute-start(bf16[1,8,16,1536]{3,2,1,0:T(8,128)(2,1)S(1)} %bitcast.57), channel_id=1, source_target_pairs={{0,4},{2,6},{4,8},{6,10},{8,12},{10,14},{12,16},{14,18},{16,20},{1... | collective-permute-start | bytes 1179656 | tf_op jit(solution)/shard_map/ppermute | solution.py:285
  128.9 0.0 copy-done.6
  128.9 0.1 dynamic-slice_convert_fusion
  129.0 0.2 reshape.50
  129.1 0.0 copy-done
  129.2 0.6 add.116
  129.8 0.1 slice_reduce_fusion.25
  129.9 0.3 slice_reduce_fusion.26
  130.2 5.0 %collective-permute-done.1 = bf16[1,8,16,1536]{3,2,1,0:T(8,128)(2,1)S(1)} collective-permute-done((bf16[1,8,16,1536]{3,2,1,0:T(8,128)(2,1)S(1)}, bf16[1,8,16,1536]{3,2,1,0:T(8,128)(2,1)S(1)}, u32[]{:S(2)}, u32[]{:S(2)}) %collective-permute-start.1) | collective-permute-done | bytes 393248 | tf_op jit(solution)/shard_map/ppermute | solution.py:286
  135.2 9.5 %collective-permute-done = bf16[1,8,16,1536]{3,2,1,0:T(8,128)(2,1)S(1)} collective-permute-done((bf16[1,8,16,1536]{3,2,1,0:T(8,128)(2,1)S(1)}, bf16[1,8,16,1536]{3,2,1,0:T(8,128)(2,1)S(1)}, u32[]{:S(2)}, u32[]{:S(2)}) %collective-permute-start) | collective-permute-done | bytes 393248 | tf_op jit(solution)/shard_map/ppermute | solution.py:285
  144.7 0.0 copy-start.5
  144.7 0.0 copy-start.7
  144.7 1.7 select_maximum_fusion
  146.4 0.0 copy-done.4
  146.5 0.0 copy-done.5
  146.5 0.0 copy-done.7
  146.5 12.9 %multiply_add_fusion = f32[4,8,16,1536]{3,2,1,0:T(8,128)S(1)} fusion(bf16[4,8,16,1536]{3,2,1,0:T(8,128)(2,1)} %bitcast.49, bf16[6,10,18,1536]{3,2,1,0:T(8,128)(2,1)S(1)} %select_maximum_fusion, bf16[1,8,16,1536]{3,2,1,0:T(8,128)(2,1)S(1)} %collective-permute-done.1, bf16[1,8,16,1536]{3,2,1,0:T(8,128)(2,1)} %copy-done.5, f32[1536]{0:T(1024)S(1)} %get-tuple-element.10, ...), kind=kLoop, calls=%fused_computation.12 | loop fusion | flops 65273856 | bytes 43425792 | tf_op jit(solution)/shard_map/add | solution.py:300
  159.4 3.3 %reshape.49 = f32[2,256,2,768]{3,2,1,0:T(2,128)} reshape(f32[4,8,16,1536]{3,2,1,0:T(8,128)S(1)} %multiply_add_fusion) | data formatting | bytes 6291456 | tf_op jit(solution)/shard_map/reshape | solution.py:303
  162.6 5.7 %fusion.8 = (f32[2,256,1,768]{3,2,1,0:T(1,128)S(1)}, f32[2,256,1,768]{3,2,1,0:T(1,128)S(1)}) fusion(f32[2,256,2,768]{3,2,1,0:T(2,128)} %reshape.49), kind=kLoop, calls=%fused_computation.57 | loop fusion | bytes 6291456 | tf_op jit(solution)/shard_map/slice | solution.py:304
  168.3 0.4 fusion.7
  168.8 0.6 collective-permute-start.2
  169.4 1.3 collective-permute-done.2
  170.7 0.1 bitcast_select_fusion.1
  170.8 0.9 pad_maximum_fusion.2
  (3 shorter events, 0.0 us)
Async XLA Ops:
  0.0 129.1 %copy-start = (f32[2,1536]{1,0:T(2,128)S(1)}, f32[2,1536]{1,0:T(2,128)}, u32[]{:S(2)}) copy-start(f32[2,1536]{1,0:T(2,128)} %param.13) | copy-start | bytes 36868
  4.9 2.7 %copy-start.2 = (f32[1,20]{1,0:T(1,128)S(1)}, f32[1,20]{1,0:T(1,128)}, u32[]{:S(2)}) copy-start(f32[1,20]{1,0:T(1,128)} %ret_ref.1) | copy-start | bytes 244
  7.6 1.1 copy-start.1
  106.1 2.9 %copy-start.3 = (bf16[8,2,144,1536]{3,2,1,0:T(8,128)(2,1)}, bf16[8,2,144,1536]{3,2,1,0:T(8,128)(2,1)S(1)}, u32[]{:S(2)}) copy-start(bf16[8,2,144,1536]{3,2,1,0:T(8,128)(2,1)S(1)} %get-tuple-element.8) | copy-start | bytes 21233668
  115.4 13.5 %copy-start.6 = (bf16[3,3,3,2,1536]{4,3,2,1,0:T(2,128)(2,1)S(1)}, bf16[3,3,3,2,1536]{4,3,2,1,0:T(2,128)(2,1)}, u32[]{:S(2)}) copy-start(bf16[3,3,3,2,1536]{4,3,2,1,0:T(2,128)(2,1)} %param.12) | copy-start | bytes 497668
  122.4 24.0 %copy-start.4 = (bf16[512,1536]{1,0:T(8,128)(2,1)}, bf16[512,1536]{1,0:T(8,128)(2,1)S(1)}, u32[]{:S(2)}) copy-start(bf16[512,1536]{1,0:T(8,128)(2,1)S(1)} %convolution_convert_fusion) | copy-start | bytes 4718596
  122.5 12.7 %collective-permute-start.1 = (bf16[1,8,16,1536]{3,2,1,0:T(8,128)(2,1)S(1)}, bf16[1,8,16,1536]{3,2,1,0:T(8,128)(2,1)S(1)}, u32[]{:S(2)}, u32[]{:S(2)}) collective-permute-start(bf16[1,8,16,1536]{3,2,1,0:T(8,128)(2,1)S(1)} %bitcast.58), channel_id=1, source_target_pairs={{4,0},{6,2},{8,4},{10,6},{12,8},{14,10},{16,12},{18,14},{20,16},{2... | collective-permute-start | bytes 1179656 | tf_op jit(solution)/shard_map/ppermute | solution.py:286
  125.9 18.9 %collective-permute-start = (bf16[1,8,16,1536]{3,2,1,0:T(8,128)(2,1)S(1)}, bf16[1,8,16,1536]{3,2,1,0:T(8,128)(2,1)S(1)}, u32[]{:S(2)}, u32[]{:S(2)}) collective-permute-start(bf16[1,8,16,1536]{3,2,1,0:T(8,128)(2,1)S(1)} %bitcast.57), channel_id=1, source_target_pairs={{0,4},{2,6},{4,8},{6,10},{8,12},{10,14},{12,16},{14,18},{16,20},{1... | collective-permute-start | bytes 1179656 | tf_op jit(solution)/shard_map/ppermute | solution.py:285
  144.7 1.7 copy-start.5
  144.7 1.7 %copy-start.7 = (f32[1536]{0:T(1024)S(1)}, f32[1536]{0:T(1024)}, u32[]{:S(2)}) copy-start(f32[1536]{0:T(1024)} %add.116) | copy-start | bytes 18436
  168.8 1.9 %collective-permute-start.2 = (bf16[256,768]{1,0:T(8,128)(2,1)S(1)}, bf16[256,768]{1,0:T(8,128)(2,1)S(1)}, u32[]{:S(2)}, u32[]{:S(2)}) collective-permute-start(bf16[256,768]{1,0:T(8,128)(2,1)S(1)} %dynamic-slice_bitcast_fusion), channel_id=1, source_target_pairs={{0,2},{2,0},{4,6},{6,4},{8,10},{10,8},{12,14},{14,12},{16,18},{18,... | collective-permute-start | bytes 1179656 | tf_op jit(solution)/shard_map/ppermute | solution.py:17

commit v2 on v1

--- a/solution.py
+++ b/solution.py
@@ -84,21 +84,33 @@
 
     started = []
 
-    def ring(hop):
-        for way in (0, 1):
-            if hop == 0:
-                continue
-            for part in halves(way, hop - 1):
-                hop_wait(way, hop - 1, part)
-        if hop < half:
+    def launch(hop):
+        for part in (0, 1):
             for way in (0, 1):
-                for part in halves(way, hop):
+                if part in halves(way, hop):
                     c = hop_copy(way, hop, part)
                     c.start()
                     started.append(c)
 
+    steps = [(hop, part) for hop in range(1, half + 1) for part in (0, 1)]
+
+    def ring(count):
+        for _ in range(min(count, len(steps))):
+            hop, part = steps.pop(0)
+            for way in (0, 1):
+                if part in halves(way, hop - 1):
+                    hop_wait(way, hop - 1, part)
+                if hop < half and part in halves(way, hop):
+                    c = hop_copy(way, hop, part)
+                    c.start()
+                    started.append(c)
+
     lane = lax.broadcasted_iota(jnp.int32, (head_dim, 128), 1)
     for h in range(heads):
+        if h == 4:
+            keep.wait()
+            across.wait()
+            launch(0)
         state = jnp.dot(kt_ref[h], v_ref[h], preferred_element_type=jnp.float32)
         keepf = jnp.full((head_dim, 128), ret_ref[0, h], jnp.float32)
         high = keepf.astype(jnp.bfloat16).astype(jnp.float32)
@@ -113,10 +125,6 @@
     ]
     for c in first:
         c.start()
-
-    keep.wait()
-    across.wait()
-    ring(0)
 
     pltpu.make_async_copy(outbox.at[spot], inbox.at[spot], lsem.at[1]).wait()
     for m in mates:
@@ -146,6 +154,7 @@
     ]
     for c in second:
         c.start()
+    ring(1)
     for o in others:
         send(tot_out, tot_in.at[o], s2.at[o], r2.at[o], device(o * BLOCK + spot)).wait_recv()
 
@@ -162,6 +171,7 @@
     ]
     for c in third:
         c.start()
+    ring(1)
     pltpu.make_async_copy(back_out.at[spot], back_in.at[spot], lsem.at[2]).wait()
     for m in mates:
         send(back_out.at[m], back_in.at[m], s3.at[m], r3.at[m], device(layer * BLOCK + m)).wait_recv()
@@ -170,7 +180,11 @@
         got = local[part, :]
         local[part, :] = factor_of(got) * back_in[j].astype(jnp.float32) + got
 
-    squares = jnp.zeros((128, 1), jnp.float32)
+    ring(1)
+    cut = heads * head_dim // groups
+    depth = w_ref.shape[1]
+    attend[...] = jnp.zeros_like(attend)
+    squares = jnp.zeros((q_ref.shape[1], 1), jnp.float32)
     column = lax.broadcasted_iota(jnp.int32, (q_ref.shape[1], 128), 1)
     for h in range(heads):
         state = local[h * head_dim : (h + 1) * head_dim, :].astype(jnp.bfloat16)
@@ -178,10 +192,16 @@
         value = numer / (numer[:, head_dim : head_dim + 1] + 0.0001)
         value = jnp.where(column < head_dim, value, 0.0)
         squares = squares + jnp.sum(value * value, axis=1, keepdims=True)
-        attend[h] = value
+        at, stop = h * head_dim, (h + 1) * head_dim
+        while at < stop:
+            block = at // cut
+            end = min(stop, (block + 1) * cut)
+            to = block * depth + at - block * cut
+            attend[:, to : to + end - at] = value[:, at - h * head_dim : end - h * head_dim]
+            at = end
+    ring(1)
     scale = lax.rsqrt(squares / (heads * head_dim) + 1e-06)
-    for h in range(heads):
-        normed[h] = (attend[h] * scale).astype(jnp.bfloat16)
+    normed[...] = (attend[...] * scale).astype(jnp.bfloat16)
     keepn = pltpu.make_async_copy(normed, nrm_ref.at[core, span], lsem.at[3])
     keepn.start()
     peers = [(span + k) % members for k in range(1, members)]
@@ -192,14 +212,13 @@
         c.start()
     cross = [send(normed, nrm_ref.at[core, span], sc.at[span], rc.at[span], twin)]
     cross[0].start()
-    ring(1)
+    ring(2)
     for p in peers:
         send(normed, nrm_ref.at[core, p], sn.at[p], rn.at[p], (grp, p)).wait_recv()
         c = send(nrm_ref.at[core, p], nrm_ref.at[core, p], sc.at[p], rc.at[p], twin)
         c.start()
         cross.append(c)
-    for hop in range(2, half + 1):
-        ring(hop)
+    ring(len(steps))
     keepn.wait()
     for p in [span] + peers:
         send(nrm_ref.at[1 - core, p], nrm_ref.at[1 - core, p], sc.at[p], rc.at[p], twin).wait_recv()
@@ -236,7 +255,7 @@
         functools.partial(fused, groups, members, heads, head_dim),
         out_shape=(
             jax.ShapeDtypeStruct((chips, 2, depth, width), bf),
-            jax.ShapeDtypeStruct((2, members, heads, tokens, 128), bf),
+            jax.ShapeDtypeStruct((2, members, tokens, groups * depth), bf),
         ),
         in_specs=[vmem, vmem, vmem, pl.BlockSpec(memory_space=pltpu.SMEM), anywhere],
         out_specs=(anywhere, anywhere),
@@ -249,8 +268,8 @@
             slabs,
             slabs,
             pltpu.VMEM((BLOCK, share, 128), jnp.float32),
-            pltpu.VMEM((heads, tokens, 128), jnp.float32),
-            pltpu.VMEM((heads, tokens, 128), bf),
+            pltpu.VMEM((tokens, groups * depth), jnp.float32),
+            pltpu.VMEM((tokens, groups * depth), bf),
             dma((BLOCK,)), dma((BLOCK,)),
             dma((layers,)), dma((layers,)),
             dma((BLOCK,)), dma((BLOCK,)),
@@ -266,10 +285,60 @@
         name="gather_and_attend",
     )(kt, v, q, retention, w)
     weight = weight.reshape(groups * depth, width)
-    normed = normed.reshape(2 * members, heads, tokens, 128)[..., :head_dim]
-    normed = normed.transpose(0, 2, 1, 3).reshape(2 * members * tokens, groups, rows)
-    normed = jnp.pad(normed, ((0, 0), (0, 0), (0, depth - rows)))
     return normed.reshape(2 * members * tokens, groups * depth), weight
+
+
+def convolve(xv, xg, bv, bg, av, ag, tv, tg, cv, cg, out, pv, pg):
+    frames = xv.shape[0]
+    for x, before, after, pad in ((xv, bv, av, pv), (xg, bg, ag, pg)):
+        pad[:, 0:1] = jnp.zeros_like(pad[:, 0:1])
+        pad[:, FH + 1 :] = jnp.zeros_like(pad[:, FH + 1 :])
+        pad[0:1, 1 : FH + 1] = before[...].astype(jnp.float32)
+        pad[frames + 1 :, 1 : FH + 1] = after[...].astype(jnp.float32)
+        pad[1 : frames + 1, 1 : FH + 1] = x[...].astype(jnp.float32)
+    tile = out.shape[-1]
+    column = lax.broadcasted_iota(jnp.int32, (FH, FW, tile), 1)
+
+    def mix(pad, taps, bias, k):
+        sums = [None, None, None]
+        for a in range(3):
+            for b in range(3):
+                slab = pad[k + a, b : b + FH]
+                for e in range(3):
+                    term = slab * taps[a * 9 + b * 3 + e : a * 9 + b * 3 + e + 1, :].reshape(1, 1, tile)
+                    sums[e] = term if sums[e] is None else sums[e] + term
+        lower = jnp.where(column > 0, pltpu.roll(sums[0], 1, 1), 0.0)
+        upper = jnp.where(column < FW - 1, pltpu.roll(sums[2], FW - 1, 1), 0.0)
+        return bias[...].reshape(1, 1, tile) + sums[1] + lower + upper
+
+    @pl.loop(0, frames)
+    def _(k):
+        value = mix(pv, tv, cv, k)
+        gate = mix(pg, tg, cg, k)
+        out[k] = (value * (gate / (1.0 + jnp.exp(-gate)))).astype(out.dtype)
+
+
+def conv_gate(grid, before, after, taps, bias):
+    frames = grid.shape[0]
+    part = grid.shape[-1] // 2
+    tile = 128 if part % 128 == 0 else part
+    operands, specs = [], []
+    for x in (grid, before, after, taps, bias):
+        lead = (0,) * (x.ndim - 1)
+        for j in (0, 1):
+            shift = j * part // tile if tile < part else 0
+            operands.append(x if tile < part else x[..., j * part : (j + 1) * part])
+            specs.append(pl.BlockSpec(x.shape[:-1] + (tile,), lambda i, lead=lead, shift=shift: lead + (i + shift,)))
+    return pl.pallas_call(
+        convolve,
+        grid=(part // tile,),
+        out_shape=jax.ShapeDtypeStruct((frames, FH, FW, part), jnp.bfloat16),
+        in_specs=specs,
+        out_specs=pl.BlockSpec((frames, FH, FW, tile), lambda i: (0, 0, 0, i)),
+        scratch_shapes=[pltpu.VMEM((frames + 2, FH + 2, FW, tile), jnp.float32)] * 2,
+        compiler_params=pltpu.CompilerParams(vmem_limit_bytes=40 * 1024 * 1024),
+        name="conv_gate",
+    )(*operands)
 
 
 def shards(queries, key_rows, value_rows, retention, up_weight, conv_weight, conv_bias):
@@ -284,24 +353,11 @@
     onward = [(i, i + 2) for i in range(groups - 2)]
     before = lax.ppermute(grid[-1:], "grp", onward)
     after = lax.ppermute(grid[:1], "grp", [(j, i) for i, j in onward])
-    extended = jnp.concatenate([before, grid, after], axis=0)
-    padded = jnp.pad(extended, ((0, 0), (1, 1), (1, 1), (0, 0)))
     taps = lax.dynamic_slice_in_dim(conv_weight, core * part, part, axis=4)
-    convolution_kernel = taps.reshape(3, 3, 3, 2 * part).astype(jnp.float32)
+    convolution_kernel = taps.reshape(27, 2 * part).astype(jnp.float32)
     bias = lax.dynamic_slice_in_dim(conv_bias, core * part, part, axis=1)
-    mixed = jnp.zeros((frames, FH, FW, 2 * part), jnp.float32) + bias.reshape(2 * part)
-    for tap_t in range(3):
-        for tap_y in range(3):
-            for tap_x in range(3):
-                visible_extent = padded[
-                    tap_t : tap_t + frames, tap_y : tap_y + FH, tap_x : tap_x + FW
-                ]
-                mixed = (
-                    mixed
-                    + visible_extent.astype(jnp.float32) * convolution_kernel[tap_t, tap_y, tap_x]
-                )
-    mixed = mixed.reshape(2, frames * FH * FW // 2, 2, part)
-    hidden = (mixed[:, :, 0] * jax.nn.silu(mixed[:, :, 1])).astype(jnp.bfloat16)
+    hidden = conv_gate(grid, before, after, convolution_kernel, bias.reshape(1, 2 * part))
+    hidden = hidden.reshape(2, frames * FH * FW // 2, part)
     mine = lax.dynamic_index_in_dim(hidden, core, 0, False)
     theirs = swap(lax.dynamic_index_in_dim(hidden, 1 - core, 0, False), groups)
     first = jnp.where(core == 0, mine, theirs)

time: 172 us -> 132 us (0.77)
  the two profiles are of different devices: /device:TPU:7 before, /device:TPU:21 now
where the time goes in v2:
time: 132 us
  Pallas kernels  96.4 us (73%)
  waiting for transfers between devices  17.3 us (13%)
  starting transfers between devices  6.64 us (5%)
  local copies, waits for them, and re-layouts  5.12 us (4%)
  matrix products  3.81 us (3%)
  other arithmetic  2.48 us (2%)
    pallas_call x1, Pallas kernels, gather_and_attend(): pl.pallas_call(functools.partial(fused, groups, members, heads, head_dim)...  88.1 us
    ppermute x1, waiting for transfers between devices, shards(): before = lax.ppermute(grid[-1:], 'grp', onward)  12.6 us
    pallas_call x1, Pallas kernels, conv_gate(): pl.pallas_call(convolve, grid=(part // tile,), out_shape=jax.ShapeDtypeSt...  8.3 us
    ppermute x1, starting transfers between devices, shards(): after = lax.ppermute(grid[:1], 'grp', [(j, i) for i, j in onward])  4.26 us
    dot_general x1, matrix products, shards(): up_vals = jnp.dot(normed, flat_weight, preferred_element_type=jnp.float32)  3.81 us
    ppermute x1, waiting for transfers between devices, shards(): after = lax.ppermute(grid[:1], 'grp', [(j, i) for i, j in onward])  3.31 us
  transfers between devices with their start and end apart: 3, of which 3 were waited for; matrix products, arithmetic and copies ran while one was open for 0% of the time, Pallas kernels for 0%

profile of v2, /device:TPU:21, one launch (start us, length us, event | category | flops | bytes accessed | tf_op | source)
XLA Modules:
  0.0 131.9 jit_solution(10702435618490599632)
XLA Ops:
  0.0 0.0 copy-start
  0.0 0.0 copy-start.4
  0.0 1.2 broadcast_maximum_fusion.1
  1.2 0.0 copy-start.3
  1.2 2.2 %copy.9 = bf16[128,20,112]{2,0,1:T(8,128)(2,1)} copy(bf16[128,20,112]{0,2,1:T(8,128)(2,1)} %bitcast.54) | data formatting | bytes 1146880 | tf_op jit(solution)/shard_map/reshape | solution.py:240
  3.4 0.1 pad.9.clone
  3.5 0.1 pad.8.clone
  3.6 0.0 copy-done.4
  3.6 0.3 copy.10
  3.9 0.0 copy-done.3
  3.9 0.6 copy.16
  4.5 0.5 reshape.39
  5.1 0.0 copy-start.2
  5.1 0.0 copy-start.1
  5.1 0.1 pad.4.w_ref
  5.2 1.0 copy-done.2
  6.2 0.2 maximum_maximum_fusion.v_ref
  6.4 0.0 copy-done.1
  6.4 88.1 %gather_and_attend.1 = (bf16[8,2,144,1536]{3,2,1,0:T(8,128)(2,1)S(1)}, bf16[2,2,128,2304]{3,2,1,0:T(8,128)(2,1)S(1)}) custom-call(bf16[20,112,128]{2,1,0:T(8,128)(2,1)S(1)} %bitcast.41, bf16[20,128,128]{2,1,0:T(8,128)(2,1)S(1)} %maximum_maximum_fusion.v_ref, bf16[20,128,112]{2,1,0:T(8,128)(2,1)S(1)} %bitcast.40, f32[1,20]{1,0:T(1,128)S(1)} %copy-done.1, ...), custom_call_target="tpu_custom_call" | custom-call | tf_op jit(solution)/shard_map/gather_and_attend/pallas_call | solution.py:254
  94.5 3.8 %convolution_convert_fusion = bf16[512,1536]{1,0:T(8,128)(2,1)S(1)} fusion(bf16[512,2304]{1,0:T(8,128)(2,1)S(1)} %bitcast.47, bf16[2304,1536]{1,0:T(8,128)(2,1)S(1)} %bitcast.46), kind=kOutput, calls=%fused_computation | convolution fusion | flops 3624665088 | bytes 11010048 | tf_op jit(solution)/shard_map/dot_general | solution.py:348
  98.4 0.0 copy-start.5
  98.4 0.1 fusion
  98.4 1.9 %collective-permute-start = (bf16[1,8,16,1536]{3,2,1,0:T(8,128)(2,1)S(1)}, bf16[1,8,16,1536]{3,2,1,0:T(8,128)(2,1)S(1)}, u32[]{:S(2)}, u32[]{:S(2)}) collective-permute-start(bf16[1,8,16,1536]{3,2,1,0:T(8,128)(2,1)S(1)} %bitcast.56), channel_id=1, source_target_pairs={{0,4},{2,6},{4,8},{6,10},{8,12},{10,14},{12,16},{14,18},{16,20},{1... | collective-permute-start | bytes 1179656 | tf_op jit(solution)/shard_map/ppermute | solution.py:354
  100.4 4.3 %collective-permute-start.1 = (bf16[1,8,16,1536]{3,2,1,0:T(8,128)(2,1)S(1)}, bf16[1,8,16,1536]{3,2,1,0:T(8,128)(2,1)S(1)}, u32[]{:S(2)}, u32[]{:S(2)}) collective-permute-start(bf16[1,8,16,1536]{3,2,1,0:T(8,128)(2,1)S(1)} %bitcast.55), channel_id=1, source_target_pairs={{4,0},{6,2},{8,4},{10,6},{12,8},{14,10},{16,12},{18,14},{20,16},{2... | collective-permute-start | bytes 1179656 | tf_op jit(solution)/shard_map/ppermute | solution.py:355
  104.6 0.0 copy-done.5
  104.7 0.1 dynamic-slice_convert_fusion
  104.7 0.1 pad.10
  104.8 0.0 copy-done
  104.9 12.6 %collective-permute-done.bv.bg = bf16[1,8,16,1536]{3,2,1,0:T(8,128)(2,1)S(1)} collective-permute-done((bf16[1,8,16,1536]{3,2,1,0:T(8,128)(2,1)S(1)}, bf16[1,8,16,1536]{3,2,1,0:T(8,128)(2,1)S(1)}, u32[]{:S(2)}, u32[]{:S(2)}) %collective-permute-start) | collective-permute-done | bytes 393248 | tf_op jit(solution)/shard_map/ppermute | solution.py:354
  117.5 3.3 %collective-permute-done.1.av.ag = bf16[1,8,16,1536]{3,2,1,0:T(8,128)(2,1)S(1)} collective-permute-done((bf16[1,8,16,1536]{3,2,1,0:T(8,128)(2,1)S(1)}, bf16[1,8,16,1536]{3,2,1,0:T(8,128)(2,1)S(1)}, u32[]{:S(2)}, u32[]{:S(2)}) %collective-permute-start.1) | collective-permute-done | bytes 393248 | tf_op jit(solution)/shard_map/ppermute | solution.py:355
  120.8 8.3 %conv_gate.1 = bf16[4,8,16,768]{3,2,1,0:T(8,128)(2,1)S(1)} custom-call(bf16[4,8,16,1536]{3,2,1,0:T(8,128)(2,1)S(1)} %bitcast.36, bf16[4,8,16,1536]{3,2,1,0:T(8,128)(2,1)S(1)} %bitcast.37, bf16[1,8,16,1536]{3,2,1,0:T(8,128)(2,1)S(1)} %collective-permute-done.bv.bg, bf16[1,8,16,1536]{3,2,1,0:T(8,128)(2,1)S(1)} %collective-permute-done.bv.bg, ...), custom_call_target="tpu_custom_call" | custom-call | tf_op jit(solution)/shard_map/conv_gate/pallas_call | solution.py:332
  129.1 0.5 collective-permute-start.2
  129.6 1.3 %collective-permute-done.2 = bf16[256,768]{1,0:T(8,128)(2,1)S(1)} collective-permute-done((bf16[256,768]{1,0:T(8,128)(2,1)S(1)}, bf16[256,768]{1,0:T(8,128)(2,1)S(1)}, u32[]{:S(2)}, u32[]{:S(2)}) %collective-permute-start.2) | collective-permute-done | bytes 393248 | tf_op jit(solution)/shard_map/ppermute | solution.py:17
  130.9 0.1 bitcast_select_fusion.1
  131.0 0.9 pad_maximum_fusion
  (6 shorter events, 0.1 us)
Async XLA Ops:
  0.0 104.8 %copy-start = (f32[2,1536]{1,0:T(2,128)S(1)}, f32[2,1536]{1,0:T(2,128)}, u32[]{:S(2)}) copy-start(f32[2,1536]{1,0:T(2,128)} %param.13) | copy-start | bytes 36868
  0.0 3.6 %copy-start.4 = (bf16[128,2240]{0,1:T(8,128)(2,1)S(1)}, bf16[128,2240]{0,1:T(8,128)(2,1)}, u32[]{:S(2)}) copy-start(bf16[128,2240]{0,1:T(8,128)(2,1)} %param.7) | copy-start | bytes 1720324
  1.2 2.8 %copy-start.3 = (bf16[140,2,1536]{2,1,0:T(2,128)(2,1)S(1)}, bf16[140,2,1536]{2,1,0:T(2,128)(2,1)}, u32[]{:S(2)}) copy-start(bf16[140,2,1536]{2,1,0:T(2,128)(2,1)} %param.11) | copy-start | bytes 2580484
  5.1 1.1 copy-start.2
  5.1 1.3 copy-start.1
  98.4 6.3 %copy-start.5 = (bf16[3,3,3,2,1536]{4,3,2,1,0:T(2,128)(2,1)S(1)}, bf16[3,3,3,2,1536]{4,3,2,1,0:T(2,128)(2,1)}, u32[]{:S(2)}) copy-start(bf16[3,3,3,2,1536]{4,3,2,1,0:T(2,128)(2,1)} %param.12) | copy-start | bytes 497668
  98.4 19.0 %collective-permute-start = (bf16[1,8,16,1536]{3,2,1,0:T(8,128)(2,1)S(1)}, bf16[1,8,16,1536]{3,2,1,0:T(8,128)(2,1)S(1)}, u32[]{:S(2)}, u32[]{:S(2)}) collective-permute-start(bf16[1,8,16,1536]{3,2,1,0:T(8,128)(2,1)S(1)} %bitcast.56), channel_id=1, source_target_pairs={{0,4},{2,6},{4,8},{6,10},{8,12},{10,14},{12,16},{14,18},{16,20},{1... | collective-permute-start | bytes 1179656 | tf_op jit(solution)/shard_map/ppermute | solution.py:354
  100.4 20.4 %collective-permute-start.1 = (bf16[1,8,16,1536]{3,2,1,0:T(8,128)(2,1)S(1)}, bf16[1,8,16,1536]{3,2,1,0:T(8,128)(2,1)S(1)}, u32[]{:S(2)}, u32[]{:S(2)}) collective-permute-start(bf16[1,8,16,1536]{3,2,1,0:T(8,128)(2,1)S(1)} %bitcast.55), channel_id=1, source_target_pairs={{4,0},{6,2},{8,4},{10,6},{12,8},{14,10},{16,12},{18,14},{20,16},{2... | collective-permute-start | bytes 1179656 | tf_op jit(solution)/shard_map/ppermute | solution.py:355
  129.1 1.8 %collective-permute-start.2 = (bf16[256,768]{1,0:T(8,128)(2,1)S(1)}, bf16[256,768]{1,0:T(8,128)(2,1)S(1)}, u32[]{:S(2)}, u32[]{:S(2)}) collective-permute-start(bf16[256,768]{1,0:T(8,128)(2,1)S(1)} %dynamic-slice_bitcast_fusion), channel_id=1, source_target_pairs={{0,2},{2,0},{4,6},{6,4},{8,10},{10,8},{12,14},{14,12},{16,18},{18,... | collective-permute-start | bytes 1179656 | tf_op jit(solution)/shard_map/ppermute | solution.py:17

commit v3 on v2

--- a/solution.py
+++ b/solution.py
@@ -19,7 +19,7 @@
 
 def fused(groups, members, heads, head_dim, kt_ref, v_ref, q_ref, ret_ref, w_ref, wg_ref, nrm_ref,
           local, outbox, inbox, tot_out, tot_in, back_out, back_in, within, attend, normed,
-          s1, r1, s2, r2, s3, r3, sw, rw, sx, rx, sn, rn, sc, rc, lsem):
+          s1, r1, s2, r2, s3, r3, sw, rw, sx, rx, sn, rn, sc, rc, se, re, st, rt, lsem):
     grp = lax.axis_index("grp")
     span = lax.axis_index("span")
     me = grp * members + span
@@ -51,6 +51,7 @@
     targets = [device(layer * BLOCK + m) for m in mates]
     targets += [device(o * BLOCK + spot) for o in others]
     targets += [right, left, twin]
+    targets += [(2 * ((chip + 1) % chips) + core, span), (2 * ((chip + chips - 1) % chips) + core, span)]
     for t in targets:
         pl.semaphore_signal(barrier, inc=1, device_id=t, device_id_type=MESH)
     pl.semaphore_wait(barrier, len(targets))
@@ -74,23 +75,28 @@
 
     def hop_copy(way, hop, part):
         source = chip_at(place - hop) if way == 0 else chip_at(place + hop)
-        at = wg_ref.at[source, part]
-        return send(at, at, sw.at[way, hop, part], rw.at[way, hop, part], right if way == 0 else left)
+        at = wg_ref.at[source, (core + part) % 2]
+        origin = w_ref.at[core] if hop == 0 and part == 0 else at
+        return send(origin, at, sw.at[way, hop, part], rw.at[way, hop, part], right if way == 0 else left)
 
     def hop_wait(way, hop, part):
         source = chip_at(place - hop - 1) if way == 0 else chip_at(place + hop + 1)
-        at = wg_ref.at[source, part]
+        at = wg_ref.at[source, (core + part) % 2]
         send(at, at, sw.at[way, hop, part], rw.at[way, hop, part], right if way == 0 else left).wait_recv()
 
     started = []
 
-    def launch(hop):
-        for part in (0, 1):
-            for way in (0, 1):
-                if part in halves(way, hop):
-                    c = hop_copy(way, hop, part)
-                    c.start()
-                    started.append(c)
+    def launch(part):
+        for way in (0, 1):
+            if part in halves(way, 0):
+                c = hop_copy(way, 0, part)
+                c.start()
+                started.append(c)
+
+    launch(0)
+
+    def slot(c, p):
+        return nrm_ref.at[1 + c * members + p]
 
     steps = [(hop, part) for hop in range(1, half + 1) for part in (0, 1)]
 
@@ -107,10 +113,9 @@
 
     lane = lax.broadcasted_iota(jnp.int32, (head_dim, 128), 1)
     for h in range(heads):
-        if h == 4:
-            keep.wait()
+        if h == 2:
             across.wait()
-            launch(0)
+            launch(1)
         state = jnp.dot(kt_ref[h], v_ref[h], preferred_element_type=jnp.float32)
         keepf = jnp.full((head_dim, 128), ret_ref[0, h], jnp.float32)
         high = keepf.astype(jnp.bfloat16).astype(jnp.float32)
@@ -181,6 +186,7 @@
         local[part, :] = factor_of(got) * back_in[j].astype(jnp.float32) + got
 
     ring(1)
+    tokens = q_ref.shape[1]
     cut = heads * head_dim // groups
     depth = w_ref.shape[1]
     attend[...] = jnp.zeros_like(attend)
@@ -202,26 +208,65 @@
     ring(1)
     scale = lax.rsqrt(squares / (heads * head_dim) + 1e-06)
     normed[...] = (attend[...] * scale).astype(jnp.bfloat16)
-    keepn = pltpu.make_async_copy(normed, nrm_ref.at[core, span], lsem.at[3])
+    keepn = pltpu.make_async_copy(normed, slot(core, span), lsem.at[3])
     keepn.start()
     peers = [(span + k) % members for k in range(1, members)]
     fourth = [
-        send(normed, nrm_ref.at[core, span], sn.at[p], rn.at[span], (grp, p)) for p in peers
+        send(normed, slot(core, span), sn.at[p], rn.at[span], (grp, p)) for p in peers
     ]
     for c in fourth:
         c.start()
-    cross = [send(normed, nrm_ref.at[core, span], sc.at[span], rc.at[span], twin)]
+    cross = [send(normed, slot(core, span), sc.at[span], rc.at[span], twin)]
     cross[0].start()
     ring(2)
     for p in peers:
-        send(normed, nrm_ref.at[core, p], sn.at[p], rn.at[p], (grp, p)).wait_recv()
-        c = send(nrm_ref.at[core, p], nrm_ref.at[core, p], sc.at[p], rc.at[p], twin)
+        send(normed, slot(core, p), sn.at[p], rn.at[p], (grp, p)).wait_recv()
+        c = send(slot(core, p), slot(core, p), sc.at[p], rc.at[p], twin)
         c.start()
         cross.append(c)
-    ring(len(steps))
     keepn.wait()
     for p in [span] + peers:
-        send(nrm_ref.at[1 - core, p], nrm_ref.at[1 - core, p], sc.at[p], rc.at[p], twin).wait_recv()
+        send(slot(1 - core, p), slot(1 - core, p), sc.at[p], rc.at[p], twin).wait_recv()
+
+    middle = tokens // 2
+    has = (chip > 0, chip < chips - 1)
+
+    def edge(side, part):
+        return nrm_ref.at[side * (2 * members + 1), pl.ds(pl.multiple_of(part * middle, middle), middle)]
+
+    def edge_copy(side):
+        source = nrm_ref.at[
+            2 * members if side == 0 else 1, pl.ds(pl.multiple_of(core * middle, middle), middle)
+        ]
+        target = (2 * (chip + (1 if side == 0 else -1)) + core, span)
+        return send(source, edge(side, core), se.at[side], re.at[side], target)
+
+    def twin_copy(side, part):
+        return send(edge(side, part), edge(side, part), st.at[side], rt.at[side], twin)
+
+    for side in (0, 1):
+        @pl.when(has[1 - side])
+        def _(side=side):
+            edge_copy(side).start()
+
+    for side in (0, 1):
+        @pl.when(has[side])
+        def _(side=side):
+            edge_copy(side).wait_recv()
+            twin_copy(side, core).start()
+
+    ring(len(steps))
+    for side in (0, 1):
+        @pl.when(has[side])
+        def _(side=side):
+            twin_copy(side, 1 - core).wait_recv()
+            twin_copy(side, core).wait_send()
+
+        @pl.when(has[1 - side])
+        def _(side=side):
+            edge_copy(side).wait_send()
+
+    keep.wait()
     for c in first + second + third + fourth + cross + started:
         c.wait_send()
 
@@ -255,7 +300,7 @@
         functools.partial(fused, groups, members, heads, head_dim),
         out_shape=(
             jax.ShapeDtypeStruct((chips, 2, depth, width), bf),
-            jax.ShapeDtypeStruct((2, members, tokens, groups * depth), bf),
+            jax.ShapeDtypeStruct((2 * members + 2, tokens, groups * depth), bf),
         ),
         in_specs=[vmem, vmem, vmem, pl.BlockSpec(memory_space=pltpu.SMEM), anywhere],
         out_specs=(anywhere, anywhere),
@@ -277,6 +322,8 @@
             dma, dma,
             dma((members,)), dma((members,)),
             dma((members,)), dma((members,)),
+            dma((2,)), dma((2,)),
+            dma((2,)), dma((2,)),
             dma((4,)),
         ],
         compiler_params=pltpu.CompilerParams(
@@ -285,17 +332,17 @@
         name="gather_and_attend",
     )(kt, v, q, retention, w)
     weight = weight.reshape(groups * depth, width)
-    return normed.reshape(2 * members * tokens, groups * depth), weight
-
-
-def convolve(xv, xg, bv, bg, av, ag, tv, tg, cv, cg, out, pv, pg):
-    frames = xv.shape[0]
-    for x, before, after, pad in ((xv, bv, av, pv), (xg, bg, ag, pg)):
+    return normed.reshape((2 * members + 2) * tokens, groups * depth), weight
+
+
+def convolve(edges, xv, xg, tv, tg, cv, cg, out, pv, pg):
+    frames = out.shape[0]
+    for x, pad in ((xv, pv), (xg, pg)):
         pad[:, 0:1] = jnp.zeros_like(pad[:, 0:1])
         pad[:, FH + 1 :] = jnp.zeros_like(pad[:, FH + 1 :])
-        pad[0:1, 1 : FH + 1] = before[...].astype(jnp.float32)
-        pad[frames + 1 :, 1 : FH + 1] = after[...].astype(jnp.float32)
-        pad[1 : frames + 1, 1 : FH + 1] = x[...].astype(jnp.float32)
+        pad[1 : frames + 1, 1 : FH + 1] = x[1 : frames + 1].astype(jnp.float32)
+        for side, k in ((0, 0), (1, frames + 1)):
+            pad[k, 1 : FH + 1] = jnp.where(edges[0, side] > 0, x[k].astype(jnp.float32), 0.0)
     tile = out.shape[-1]
     column = lax.broadcasted_iota(jnp.int32, (FH, FW, tile), 1)
 
@@ -318,12 +365,12 @@
         out[k] = (value * (gate / (1.0 + jnp.exp(-gate)))).astype(out.dtype)
 
 
-def conv_gate(grid, before, after, taps, bias):
-    frames = grid.shape[0]
+def conv_gate(edges, grid, taps, bias):
+    frames = grid.shape[0] - 2
     part = grid.shape[-1] // 2
     tile = 128 if part % 128 == 0 else part
-    operands, specs = [], []
-    for x in (grid, before, after, taps, bias):
+    operands, specs = [edges], [pl.BlockSpec(memory_space=pltpu.SMEM)]
+    for x in (grid, taps, bias):
         lead = (0,) * (x.ndim - 1)
         for j in (0, 1):
             shift = j * part // tile if tile < part else 0
@@ -348,15 +395,14 @@
     up_vals = jnp.dot(normed, flat_weight, preferred_element_type=jnp.float32)
     up_vals = up_vals.astype(jnp.bfloat16)
     part = flat_weight.shape[1] // 2
-    frames = up_vals.shape[0] // (FH * FW)
-    grid = up_vals.reshape(frames, FH, FW, 2 * part)
-    onward = [(i, i + 2) for i in range(groups - 2)]
-    before = lax.ppermute(grid[-1:], "grp", onward)
-    after = lax.ppermute(grid[:1], "grp", [(j, i) for i, j in onward])
+    frames = up_vals.shape[0] // (FH * FW) - 2
+    grid = up_vals.reshape(frames + 2, FH, FW, 2 * part)
+    group = lax.axis_index("grp")
+    edges = jnp.stack([group >= 2, group < groups - 2]).astype(jnp.int32).reshape(1, 2)
     taps = lax.dynamic_slice_in_dim(conv_weight, core * part, part, axis=4)
     convolution_kernel = taps.reshape(27, 2 * part).astype(jnp.float32)
     bias = lax.dynamic_slice_in_dim(conv_bias, core * part, part, axis=1)
-    hidden = conv_gate(grid, before, after, convolution_kernel, bias.reshape(1, 2 * part))
+    hidden = conv_gate(edges, grid, convolution_kernel, bias.reshape(1, 2 * part))
     hidden = hidden.reshape(2, frames * FH * FW // 2, part)
     mine = lax.dynamic_index_in_dim(hidden, core, 0, False)
     theirs = swap(lax.dynamic_index_in_dim(hidden, 1 - core, 0, False), groups)

time: 132 us -> 127 us (0.962)
  the two profiles are of different devices: /device:TPU:21 before, /device:TPU:7 now
where the time goes in v3:
time: 127 us
  Pallas kernels  111 us (87%)
  matrix products  5.85 us (5%)
  local copies, waits for them, and re-layouts  3.99 us (3%)
  other arithmetic  3.68 us (3%)
  waiting for transfers between devices  1.35 us (1%)
    pallas_call x1, Pallas kernels, gather_and_attend(): pl.pallas_call(functools.partial(fused, groups, members, heads, head_dim)...  103 us
    pallas_call x1, Pallas kernels, conv_gate(): pl.pallas_call(convolve, grid=(part // tile,), out_shape=jax.ShapeDtypeSt...  8.4 us
    dot_general x1, matrix products, shards(): up_vals = jnp.dot(normed, flat_weight, preferred_element_type=jnp.float32)  5.85 us
  transfers between devices with their start and end apart: 1, of which 1 were waited for; matrix products, arithmetic and copies ran while one was open for 0% of the time, Pallas kernels for 0%

profile of v3, /device:TPU:7, one launch (start us, length us, event | category | flops | bytes accessed | tf_op | source)
XLA Modules:
  0.0 126.9 jit_solution(14904356715081487680)
XLA Ops:
  0.0 0.0 copy-start
  0.0 0.0 copy-start.3
  0.0 0.0 copy-start.2
  0.0 1.2 broadcast_maximum_fusion.1
  1.2 2.1 %copy.9 = bf16[128,20,112]{2,0,1:T(8,128)(2,1)} copy(bf16[128,20,112]{0,2,1:T(8,128)(2,1)} %bitcast.54) | data formatting | bytes 1146880 | tf_op jit(solution)/shard_map/reshape | solution.py:285
  3.4 0.1 pad.9.clone
  3.4 0.1 pad.8.clone
  3.5 0.0 copy-done.3
  3.6 0.3 copy.10
  3.9 0.0 copy-done.2
  3.9 0.0 copy-start.4
  3.9 0.6 copy.16
  4.5 0.5 reshape.69
  5.1 0.0 copy-start.1
  5.1 0.1 pad.4.w_ref
  5.2 0.0 copy-done.4
  5.2 0.1 dynamic-slice_convert_fusion
  5.3 0.1 pad.12
  5.4 0.0 copy-done
  5.4 0.1 add_convert_fusion.edges
  5.5 1.3 %maximum_maximum_fusion.v_ref = bf16[20,128,128]{2,1,0:T(8,128)(2,1)S(1)} fusion(bf16[20,128,112]{2,1,0:T(8,128)(2,1)} %bitcast.49, bf16[128]{0:T(256)(128)(2,1)S(1)} %pad.9.clone, bf16[128]{0:T(256)(128)(2,1)S(1)} %pad.8.clone), kind=kLoop, calls=%fused_computation.3 | loop fusion | flops 1966080 | bytes 1229312 | tf_op jit(solution)/shard_map/concatenate | solution.py:288
  6.8 0.0 copy-done.1
  6.8 103.0 %gather_and_attend.1 = (bf16[8,2,144,1536]{3,2,1,0:T(8,128)(2,1)S(1)}, bf16[6,128,2304]{2,1,0:T(8,128)(2,1)S(1)}) custom-call(bf16[20,112,128]{2,1,0:T(8,128)(2,1)S(1)} %bitcast.41, bf16[20,128,128]{2,1,0:T(8,128)(2,1)S(1)} %maximum_maximum_fusion.v_ref, bf16[20,128,112]{2,1,0:T(8,128)(2,1)S(1)} %bitcast.40, f32[1,20]{1,0:T(1,128)S(1)} %copy-done.1, ...), custom_call_target="tpu_custom_call" | custom-call | tf_op jit(solution)/shard_map/gather_and_attend/pallas_call | solution.py:299
  109.8 5.9 %convolution_convert_fusion = bf16[768,1536]{1,0:T(8,128)(2,1)S(1)} fusion(bf16[768,2304]{1,0:T(8,128)(2,1)S(1)} %bitcast.47, bf16[2304,1536]{1,0:T(8,128)(2,1)S(1)} %bitcast.46), kind=kOutput, calls=%fused_computation | convolution fusion | flops 5436997632 | bytes 12976128 | tf_op jit(solution)/shard_map/dot_general | solution.py:395
  115.7 8.4 %conv_gate.1 = bf16[4,8,16,768]{3,2,1,0:T(8,128)(2,1)S(1)} custom-call(s32[1,2]{1,0:T(1,128)S(1)} %add_convert_fusion.edges, bf16[6,8,16,1536]{3,2,1,0:T(8,128)(2,1)S(1)} %bitcast.36, bf16[6,8,16,1536]{3,2,1,0:T(8,128)(2,1)S(1)} %bitcast.37, f32[27,1536]{1,0:T(8,128)S(1)} %bitcast.42, f32[27,1536]{1,0:T(8,128)S(1)} %bitcast.43, f32[1,1536]{1,0:T(1,128)S(1)} %bitcast.44, ...), custom_call_target="tpu_custom_call" | custom-call | tf_op jit(solution)/shard_map/conv_gate/pallas_call | solution.py:379
  124.2 0.4 collective-permute-start
  124.6 1.3 %collective-permute-done = bf16[256,768]{1,0:T(8,128)(2,1)S(1)} collective-permute-done((bf16[256,768]{1,0:T(8,128)(2,1)S(1)}, bf16[256,768]{1,0:T(8,128)(2,1)S(1)}, u32[]{:S(2)}, u32[]{:S(2)}) %collective-permute-start) | collective-permute-done | bytes 393248 | tf_op jit(solution)/shard_map/ppermute | solution.py:17
  126.0 0.1 bitcast_select_fusion.1
  126.0 0.9 pad_maximum_fusion
  (6 shorter events, 0.1 us)
Async XLA Ops:
  0.0 5.4 %copy-start = (f32[2,1536]{1,0:T(2,128)S(1)}, f32[2,1536]{1,0:T(2,128)}, u32[]{:S(2)}) copy-start(f32[2,1536]{1,0:T(2,128)} %param.13) | copy-start | bytes 36868
  0.0 3.5 %copy-start.3 = (bf16[128,2240]{0,1:T(8,128)(2,1)S(1)}, bf16[128,2240]{0,1:T(8,128)(2,1)}, u32[]{:S(2)}) copy-start(bf16[128,2240]{0,1:T(8,128)(2,1)} %param.7) | copy-start | bytes 1720324
  0.0 3.9 %copy-start.2 = (bf16[140,2,1536]{2,1,0:T(2,128)(2,1)S(1)}, bf16[140,2,1536]{2,1,0:T(2,128)(2,1)}, u32[]{:S(2)}) copy-start(bf16[140,2,1536]{2,1,0:T(2,128)(2,1)} %param.11) | copy-start | bytes 2580484
  3.9 1.3 copy-start.4
  5.1 1.7 %copy-start.1 = (f32[1,20]{1,0:T(1,128)S(1)}, f32[1,20]{1,0:T(1,128)}, u32[]{:S(2)}) copy-start(f32[1,20]{1,0:T(1,128)} %ret_ref.1) | copy-start | bytes 244
  124.2 1.8 %collective-permute-start = (bf16[256,768]{1,0:T(8,128)(2,1)S(1)}, bf16[256,768]{1,0:T(8,128)(2,1)S(1)}, u32[]{:S(2)}, u32[]{:S(2)}) collective-permute-start(bf16[256,768]{1,0:T(8,128)(2,1)S(1)} %dynamic-slice_bitcast_fusion), channel_id=1, source_target_pairs={{0,2},{2,0},{4,6},{6,4},{8,10},{10,8},{12,14},{14,12},{16,18},{18,... | collective-permute-start | bytes 1179656 | tf_op jit(solution)/shard_map/ppermute | solution.py:17

commit v4 on v3

--- a/solution.py
+++ b/solution.py
@@ -218,7 +218,7 @@
         c.start()
     cross = [send(normed, slot(core, span), sc.at[span], rc.at[span], twin)]
     cross[0].start()
-    ring(2)
+    ring(1)
     for p in peers:
         send(normed, slot(core, p), sn.at[p], rn.at[p], (grp, p)).wait_recv()
         c = send(slot(core, p), slot(core, p), sc.at[p], rc.at[p], twin)
@@ -248,6 +248,8 @@
         @pl.when(has[1 - side])
         def _(side=side):
             edge_copy(side).start()
+
+    ring(1)
 
     for side in (0, 1):
         @pl.when(has[side])
@@ -368,7 +370,7 @@
 def conv_gate(edges, grid, taps, bias):
     frames = grid.shape[0] - 2
     part = grid.shape[-1] // 2
-    tile = 128 if part % 128 == 0 else part
+    tile = 256 if part % 256 == 0 else 128 if part % 128 == 0 else part
     operands, specs = [edges], [pl.BlockSpec(memory_space=pltpu.SMEM)]
     for x in (grid, taps, bias):
         lead = (0,) * (x.ndim - 1)

time: 127 us -> 123 us (0.969)
  Pallas kernels: 111 us -> 108 us
    pallas_call x1, Pallas kernels: 103 us -> 99.7 us  [gather_and_attend(): pl.pallas_call(functools.partial(fused, groups, members, heads, head_dim)...]
where the time goes in v4:
time: 123 us
  Pallas kernels  108 us (88%)
  matrix products  5.85 us (5%)
  local copies, waits for them, and re-layouts  3.99 us (3%)
  other arithmetic  3.68 us (3%)
  waiting for transfers between devices  1.7 us (1%)
    pallas_call x1, Pallas kernels, gather_and_attend(): pl.pallas_call(functools.partial(fused, groups, members, heads, head_dim)...  99.7 us
    pallas_call x1, Pallas kernels, conv_gate(): pl.pallas_call(convolve, grid=(part // tile,), out_shape=jax.ShapeDtypeSt...  8.01 us
    dot_general x1, matrix products, shards(): up_vals = jnp.dot(normed, flat_weight, preferred_element_type=jnp.float32)  5.85 us
  transfers between devices with their start and end apart: 1, of which 1 were waited for; matrix products, arithmetic and copies ran while one was open for 0% of the time, Pallas kernels for 0%

profile of v4, /device:TPU:7, one launch (start us, length us, event | category | flops | bytes accessed | tf_op | source)
XLA Modules:
  0.0 123.3 jit_solution(12087201501261057272)
XLA Ops:
  0.0 0.0 copy-start
  0.0 0.0 copy-start.3
  0.0 0.0 copy-start.2
  0.0 1.2 broadcast_maximum_fusion.1
  1.2 2.1 %copy.9 = bf16[128,20,112]{2,0,1:T(8,128)(2,1)} copy(bf16[128,20,112]{0,2,1:T(8,128)(2,1)} %bitcast.54) | data formatting | bytes 1146880 | tf_op jit(solution)/shard_map/reshape | solution.py:287
  3.4 0.1 pad.9.clone
  3.4 0.1 pad.8.clone
  3.5 0.0 copy-done.3
  3.6 0.3 copy.10
  3.9 0.0 copy-done.2
  3.9 0.0 copy-start.4
  3.9 0.6 copy.16
  4.5 0.5 reshape.69
  5.1 0.0 copy-start.1
  5.1 0.1 pad.4.w_ref
  5.2 0.0 copy-done.4
  5.2 0.1 dynamic-slice_convert_fusion
  5.3 0.1 pad.12
  5.4 0.0 copy-done
  5.4 0.1 add_convert_fusion.edges
  5.5 1.3 %maximum_maximum_fusion.v_ref = bf16[20,128,128]{2,1,0:T(8,128)(2,1)S(1)} fusion(bf16[20,128,112]{2,1,0:T(8,128)(2,1)} %bitcast.49, bf16[128]{0:T(256)(128)(2,1)S(1)} %pad.9.clone, bf16[128]{0:T(256)(128)(2,1)S(1)} %pad.8.clone), kind=kLoop, calls=%fused_computation.3 | loop fusion | flops 1966080 | bytes 1229312 | tf_op jit(solution)/shard_map/concatenate | solution.py:290
  6.8 0.0 copy-done.1
  6.8 99.7 %gather_and_attend.1 = (bf16[8,2,144,1536]{3,2,1,0:T(8,128)(2,1)S(1)}, bf16[6,128,2304]{2,1,0:T(8,128)(2,1)S(1)}) custom-call(bf16[20,112,128]{2,1,0:T(8,128)(2,1)S(1)} %bitcast.41, bf16[20,128,128]{2,1,0:T(8,128)(2,1)S(1)} %maximum_maximum_fusion.v_ref, bf16[20,128,112]{2,1,0:T(8,128)(2,1)S(1)} %bitcast.40, f32[1,20]{1,0:T(1,128)S(1)} %copy-done.1, ...), custom_call_target="tpu_custom_call" | custom-call | tf_op jit(solution)/shard_map/gather_and_attend/pallas_call | solution.py:301
  106.6 5.9 %convolution_convert_fusion = bf16[768,1536]{1,0:T(8,128)(2,1)S(1)} fusion(bf16[768,2304]{1,0:T(8,128)(2,1)S(1)} %bitcast.47, bf16[2304,1536]{1,0:T(8,128)(2,1)S(1)} %bitcast.46), kind=kOutput, calls=%fused_computation | convolution fusion | flops 5436997632 | bytes 12976128 | tf_op jit(solution)/shard_map/dot_general | solution.py:397
  112.4 8.0 %conv_gate.1 = bf16[4,8,16,768]{3,2,1,0:T(8,128)(2,1)S(1)} custom-call(s32[1,2]{1,0:T(1,128)S(1)} %add_convert_fusion.edges, bf16[6,8,16,1536]{3,2,1,0:T(8,128)(2,1)S(1)} %bitcast.36, bf16[6,8,16,1536]{3,2,1,0:T(8,128)(2,1)S(1)} %bitcast.37, f32[27,1536]{1,0:T(8,128)S(1)} %bitcast.42, f32[27,1536]{1,0:T(8,128)S(1)} %bitcast.43, f32[1,1536]{1,0:T(1,128)S(1)} %bitcast.44, ...), custom_call_target="tpu_custom_call" | custom-call | tf_op jit(solution)/shard_map/conv_gate/pallas_call | solution.py:381
  120.5 0.1 collective-permute-start
  120.6 1.7 %collective-permute-done = bf16[256,768]{1,0:T(8,128)(2,1)S(1)} collective-permute-done((bf16[256,768]{1,0:T(8,128)(2,1)S(1)}, bf16[256,768]{1,0:T(8,128)(2,1)S(1)}, u32[]{:S(2)}, u32[]{:S(2)}) %collective-permute-start) | collective-permute-done | bytes 393248 | tf_op jit(solution)/shard_map/ppermute | solution.py:17
  122.3 0.1 bitcast_select_fusion.1
  122.3 0.9 pad_maximum_fusion
  (6 shorter events, 0.1 us)
Async XLA Ops:
  0.0 5.4 %copy-start = (f32[2,1536]{1,0:T(2,128)S(1)}, f32[2,1536]{1,0:T(2,128)}, u32[]{:S(2)}) copy-start(f32[2,1536]{1,0:T(2,128)} %param.13) | copy-start | bytes 36868
  0.0 3.5 %copy-start.3 = (bf16[128,2240]{0,1:T(8,128)(2,1)S(1)}, bf16[128,2240]{0,1:T(8,128)(2,1)}, u32[]{:S(2)}) copy-start(bf16[128,2240]{0,1:T(8,128)(2,1)} %param.7) | copy-start | bytes 1720324
  0.0 3.9 %copy-start.2 = (bf16[140,2,1536]{2,1,0:T(2,128)(2,1)S(1)}, bf16[140,2,1536]{2,1,0:T(2,128)(2,1)}, u32[]{:S(2)}) copy-start(bf16[140,2,1536]{2,1,0:T(2,128)(2,1)} %param.11) | copy-start | bytes 2580484
  3.9 1.3 %copy-start.4 = (bf16[3,3,3,2,1536]{4,3,2,1,0:T(2,128)(2,1)S(1)}, bf16[3,3,3,2,1536]{4,3,2,1,0:T(2,128)(2,1)}, u32[]{:S(2)}) copy-start(bf16[3,3,3,2,1536]{4,3,2,1,0:T(2,128)(2,1)} %param.12) | copy-start | bytes 497668
  5.1 1.7 %copy-start.1 = (f32[1,20]{1,0:T(1,128)S(1)}, f32[1,20]{1,0:T(1,128)}, u32[]{:S(2)}) copy-start(f32[1,20]{1,0:T(1,128)} %ret_ref.1) | copy-start | bytes 244
  120.5 1.8 %collective-permute-start = (bf16[256,768]{1,0:T(8,128)(2,1)S(1)}, bf16[256,768]{1,0:T(8,128)(2,1)S(1)}, u32[]{:S(2)}, u32[]{:S(2)}) collective-permute-start(bf16[256,768]{1,0:T(8,128)(2,1)S(1)} %dynamic-slice_bitcast_fusion), channel_id=1, source_target_pairs={{0,2},{2,0},{4,6},{6,4},{8,10},{10,8},{12,14},{14,12},{16,18},{18,... | collective-permute-start | bytes 1179656 | tf_op jit(solution)/shard_map/ppermute | solution.py:17

commit v5 on v4

--- a/solution.py
+++ b/solution.py
@@ -113,9 +113,6 @@
 
     lane = lax.broadcasted_iota(jnp.int32, (head_dim, 128), 1)
     for h in range(heads):
-        if h == 2:
-            across.wait()
-            launch(1)
         state = jnp.dot(kt_ref[h], v_ref[h], preferred_element_type=jnp.float32)
         keepf = jnp.full((head_dim, 128), ret_ref[0, h], jnp.float32)
         high = keepf.astype(jnp.bfloat16).astype(jnp.float32)
@@ -130,6 +127,8 @@
     ]
     for c in first:
         c.start()
+    across.wait()
+    launch(1)
 
     pltpu.make_async_copy(outbox.at[spot], inbox.at[spot], lsem.at[1]).wait()
     for m in mates:

time: 123 us -> 123 us (level)
  Pallas kernels: 108 us -> 106 us
  starting transfers between devices: 0.07 us -> 1.61 us
    pallas_call x1, Pallas kernels: 99.7 us -> 97.9 us  [gather_and_attend(): pl.pallas_call(functools.partial(fused, groups, members, heads, head_dim)...]
    ppermute x1, starting transfers between devices: 0.07 us -> 1.61 us  [swap(): return lax.ppermute(x, 'grp', [(i, i ^ 1) for i in range(groups)])]
where the time goes in v5:
time: 123 us
  Pallas kernels  106 us (86%)
  matrix products  5.86 us (5%)
  local copies, waits for them, and re-layouts  3.99 us (3%)
  other arithmetic  3.68 us (3%)
  starting transfers between devices  1.61 us (1%)
  waiting for transfers between devices  1.35 us (1%)
    pallas_call x1, Pallas kernels, gather_and_attend(): pl.pallas_call(functools.partial(fused, groups, members, heads, head_dim)...  97.9 us
    pallas_call x1, Pallas kernels, conv_gate(): pl.pallas_call(convolve, grid=(part // tile,), out_shape=jax.ShapeDtypeSt...  8.01 us
    dot_general x1, matrix products, shards(): up_vals = jnp.dot(normed, flat_weight, preferred_element_type=jnp.float32)  5.86 us
  transfers between devices with their start and end apart: 1, of which 1 were waited for; matrix products, arithmetic and copies ran while one was open for 0% of the time, Pallas kernels for 0%

profile of v5, /device:TPU:7, one launch (start us, length us, event | category | flops | bytes accessed | tf_op | source)
XLA Modules:
  0.0 122.6 jit_solution(15536812315085970899)
XLA Ops:
  0.0 0.0 copy-start
  0.0 0.0 copy-start.3
  0.0 0.0 copy-start.2
  0.0 1.2 broadcast_maximum_fusion.1
  1.2 2.1 %copy.9 = bf16[128,20,112]{2,0,1:T(8,128)(2,1)} copy(bf16[128,20,112]{0,2,1:T(8,128)(2,1)} %bitcast.54) | data formatting | bytes 1146880 | tf_op jit(solution)/shard_map/reshape | solution.py:286
  3.4 0.1 pad.9.clone
  3.4 0.1 pad.8.clone
  3.5 0.0 copy-done.3
  3.6 0.3 copy.10
  3.9 0.0 copy-done.2
  3.9 0.0 copy-start.4
  3.9 0.6 copy.16
  4.5 0.5 reshape.69
  5.1 0.0 copy-start.1
  5.1 0.1 pad.4.w_ref
  5.2 0.0 copy-done.4
  5.2 0.1 dynamic-slice_convert_fusion
  5.3 0.1 pad.12
  5.4 0.0 copy-done
  5.4 0.1 add_convert_fusion.edges
  5.5 1.3 %maximum_maximum_fusion.v_ref = bf16[20,128,128]{2,1,0:T(8,128)(2,1)S(1)} fusion(bf16[20,128,112]{2,1,0:T(8,128)(2,1)} %bitcast.49, bf16[128]{0:T(256)(128)(2,1)S(1)} %pad.9.clone, bf16[128]{0:T(256)(128)(2,1)S(1)} %pad.8.clone), kind=kLoop, calls=%fused_computation.3 | loop fusion | flops 1966080 | bytes 1229312 | tf_op jit(solution)/shard_map/concatenate | solution.py:289
  6.8 0.0 copy-done.1
  6.8 97.9 %gather_and_attend.1 = (bf16[8,2,144,1536]{3,2,1,0:T(8,128)(2,1)S(1)}, bf16[6,128,2304]{2,1,0:T(8,128)(2,1)S(1)}) custom-call(bf16[20,112,128]{2,1,0:T(8,128)(2,1)S(1)} %bitcast.41, bf16[20,128,128]{2,1,0:T(8,128)(2,1)S(1)} %maximum_maximum_fusion.v_ref, bf16[20,128,112]{2,1,0:T(8,128)(2,1)S(1)} %bitcast.40, f32[1,20]{1,0:T(1,128)S(1)} %copy-done.1, ...), custom_call_target="tpu_custom_call" | custom-call | tf_op jit(solution)/shard_map/gather_and_attend/pallas_call | solution.py:300
  104.7 5.9 %convolution_convert_fusion = bf16[768,1536]{1,0:T(8,128)(2,1)S(1)} fusion(bf16[768,2304]{1,0:T(8,128)(2,1)S(1)} %bitcast.47, bf16[2304,1536]{1,0:T(8,128)(2,1)S(1)} %bitcast.46), kind=kOutput, calls=%fused_computation | convolution fusion | flops 5436997632 | bytes 12976128 | tf_op jit(solution)/shard_map/dot_general | solution.py:396
  110.6 8.0 %conv_gate.1 = bf16[4,8,16,768]{3,2,1,0:T(8,128)(2,1)S(1)} custom-call(s32[1,2]{1,0:T(1,128)S(1)} %add_convert_fusion.edges, bf16[6,8,16,1536]{3,2,1,0:T(8,128)(2,1)S(1)} %bitcast.36, bf16[6,8,16,1536]{3,2,1,0:T(8,128)(2,1)S(1)} %bitcast.37, f32[27,1536]{1,0:T(8,128)S(1)} %bitcast.42, f32[27,1536]{1,0:T(8,128)S(1)} %bitcast.43, f32[1,1536]{1,0:T(1,128)S(1)} %bitcast.44, ...), custom_call_target="tpu_custom_call" | custom-call | tf_op jit(solution)/shard_map/conv_gate/pallas_call | solution.py:380
  118.6 1.6 %collective-permute-start = (bf16[256,768]{1,0:T(8,128)(2,1)S(1)}, bf16[256,768]{1,0:T(8,128)(2,1)S(1)}, u32[]{:S(2)}, u32[]{:S(2)}) collective-permute-start(bf16[256,768]{1,0:T(8,128)(2,1)S(1)} %dynamic-slice_bitcast_fusion), channel_id=1, source_target_pairs={{0,2},{2,0},{4,6},{6,4},{8,10},{10,8},{12,14},{14,12},{16,18},{18,... | collective-permute-start | bytes 1179656 | tf_op jit(solution)/shard_map/ppermute | solution.py:17
  120.2 1.3 %collective-permute-done = bf16[256,768]{1,0:T(8,128)(2,1)S(1)} collective-permute-done((bf16[256,768]{1,0:T(8,128)(2,1)S(1)}, bf16[256,768]{1,0:T(8,128)(2,1)S(1)}, u32[]{:S(2)}, u32[]{:S(2)}) %collective-permute-start) | collective-permute-done | bytes 393248 | tf_op jit(solution)/shard_map/ppermute | solution.py:17
  121.6 0.1 bitcast_select_fusion.1
  121.6 0.9 pad_maximum_fusion
  (6 shorter events, 0.1 us)
Async XLA Ops:
  0.0 5.4 %copy-start = (f32[2,1536]{1,0:T(2,128)S(1)}, f32[2,1536]{1,0:T(2,128)}, u32[]{:S(2)}) copy-start(f32[2,1536]{1,0:T(2,128)} %param.13) | copy-start | bytes 36868
  0.0 3.5 %copy-start.3 = (bf16[128,2240]{0,1:T(8,128)(2,1)S(1)}, bf16[128,2240]{0,1:T(8,128)(2,1)}, u32[]{:S(2)}) copy-start(bf16[128,2240]{0,1:T(8,128)(2,1)} %param.7) | copy-start | bytes 1720324
  0.0 3.9 %copy-start.2 = (bf16[140,2,1536]{2,1,0:T(2,128)(2,1)S(1)}, bf16[140,2,1536]{2,1,0:T(2,128)(2,1)}, u32[]{:S(2)}) copy-start(bf16[140,2,1536]{2,1,0:T(2,128)(2,1)} %param.11) | copy-start | bytes 2580484
  3.9 1.3 %copy-start.4 = (bf16[3,3,3,2,1536]{4,3,2,1,0:T(2,128)(2,1)S(1)}, bf16[3,3,3,2,1536]{4,3,2,1,0:T(2,128)(2,1)}, u32[]{:S(2)}) copy-start(bf16[3,3,3,2,1536]{4,3,2,1,0:T(2,128)(2,1)} %param.12) | copy-start | bytes 497668
  5.1 1.7 %copy-start.1 = (f32[1,20]{1,0:T(1,128)S(1)}, f32[1,20]{1,0:T(1,128)}, u32[]{:S(2)}) copy-start(f32[1,20]{1,0:T(1,128)} %ret_ref.1) | copy-start | bytes 244
  118.6 3.0 %collective-permute-start = (bf16[256,768]{1,0:T(8,128)(2,1)S(1)}, bf16[256,768]{1,0:T(8,128)(2,1)S(1)}, u32[]{:S(2)}, u32[]{:S(2)}) collective-permute-start(bf16[256,768]{1,0:T(8,128)(2,1)S(1)} %dynamic-slice_bitcast_fusion), channel_id=1, source_target_pairs={{0,2},{2,0},{4,6},{6,4},{8,10},{10,8},{12,14},{14,12},{16,18},{18,... | collective-permute-start | bytes 1179656 | tf_op jit(solution)/shard_map/ppermute | solution.py:17
